TPU v7x, 256 devices: a whole 4x4x8 slice. The times are simulated.
256 devices in a mesh: ctx: 16 (over y, z_hi, core), ch: 16 (over z_lo, x).
Axes of the slice: x: 4, y: 4, z: 8 (z_hi: 2, z_lo: 4; z = z_hi * 4 + z_lo), core: 2. Of those that a mesh axis runs over, the one named last changes fastest.
Arguments:
- streams: bfloat16 [3, 256, 524288], P(None, 'ch', 'ctx'), parts along dimension 1, may hold values from -6 to 6
- short_weight: bfloat16 [3, 256, 3], P(None, 'ch'), parts along dimension 1, may hold values from -3.5 to 3.5
- gate_bias: float32 [256], P('ch'), parts along dimension 0, may hold values from -1 to 1
- filter_spectrum: float32 [2, 256, 512, 2048], P(None, 'ch', None, 'ctx'), parts along dimension 1, may hold values from -6 to 6
Outputs:
- gated: bfloat16 [256, 524288], P('ch', 'ctx'), parts along dimension 0
There are 16 independent parts, one for each index of `ch`. A program takes and returns all parts, laid end to end along the dimension named above; each array names one. Nothing has to cross between parts.
All inputs are finite; a program needn't handle non-finite values.
Results may differ from a plain program's by a relative error of at most 0.01.
Values may be sent and summed in bfloat16 or wider, within the bound.
No kernel may reach another device: no remote copies, remote signals or barrier semaphores. Data moves between devices by JAX's collectives and lax.ppermute only.
A program may use at most 192 MiB of HBM per device.

v0:
```python
import math

import jax
import jax.numpy as jnp
from jax import lax
from jax.sharding import PartitionSpec as P

FACTOR_A = 2048
FACTOR_B = 512
SHORT_TAPS = 3


def shifted(block, axis, distance):
    devices = range(lax.axis_size(axis))
    route = [(i - distance, i) for i in devices if i - distance in devices]
    return lax.ppermute(block, axis, route)


def tables(row_start, row_count, col_start, col_count, size):
    row_index = row_start + jnp.arange(row_count, dtype=jnp.int32)[:, None]
    col_index = col_start + jnp.arange(col_count, dtype=jnp.int32)[None, :]
    turns = row_index * col_index % size
    angle = turns.astype(jnp.float32) * (2.0 * math.pi / size)
    return (jnp.cos(angle), -jnp.sin(angle))


def featurize(padded, short_weight, length):
    weights = short_weight.astype(jnp.float32)
    tap_count = weights.shape[2]
    summed = jnp.zeros(padded.shape[:2] + (length,), jnp.float32)
    for offset in range(tap_count):
        begin = tap_count - 1 - offset
        summed = summed + weights[:, :, offset, None] * padded[:, :, begin : begin + length]
    return summed


def mult(form, left, right):
    return jnp.einsum(form, left, right, preferred_element_type=jnp.float32)


def per_device(streams, short_weight, gate_bias, filter_spectrum):
    ctx_count = lax.axis_size("ctx")
    ctx_place = lax.axis_index("ctx")
    channels = streams.shape[1]
    length = streams.shape[2]
    half_rows = FACTOR_A // 2
    points = FACTOR_A * FACTOR_B
    block_cols = FACTOR_B // ctx_count
    freq_cols = FACTOR_A // ctx_count
    inverse_scale = 1.0 / points
    rim_rows = shifted(streams[:, :, length - (SHORT_TAPS - 1) :], "ctx", 1)
    padded = jnp.concatenate([rim_rows, streams], axis=2).astype(jnp.float32)
    mixed_streams = featurize(padded, short_weight, length)
    product = (mixed_streams[0] * mixed_streams[2]).astype(jnp.bfloat16)
    gate_stream = mixed_streams[1]
    grid_rows = product.reshape(channels, length // FACTOR_B, FACTOR_B)
    cos_a, sin_a = tables(0, half_rows, 0, FACTOR_A, FACTOR_A)
    cos_a = cos_a.astype(jnp.bfloat16)
    sin_a = sin_a.astype(jnp.bfloat16)
    fwd_c, fwd_s = tables(ctx_place * block_cols, block_cols, 0, FACTOR_A, points)
    pieces = lax.all_to_all(grid_rows, "ctx", split_axis=2, concat_axis=1, tiled=True)
    real_part = mult("cab,ak->cbk", pieces, cos_a)
    imag_part = mult("cab,ak->cbk", pieces, sin_a)
    mid_real = (real_part * fwd_c - imag_part * fwd_s).astype(jnp.bfloat16)
    mid_imag = (real_part * fwd_s + imag_part * fwd_c).astype(jnp.bfloat16)
    cos_b, sin_b = tables(0, FACTOR_B, 0, FACTOR_B, FACTOR_B)
    cos_b = cos_b.astype(jnp.bfloat16)
    sin_b = sin_b.astype(jnp.bfloat16)
    part_real = lax.all_to_all(mid_real, "ctx", split_axis=2, concat_axis=1, tiled=True)
    part_imag = lax.all_to_all(mid_imag, "ctx", split_axis=2, concat_axis=1, tiled=True)
    spec_real = mult("cbk,bq->cqk", part_real, cos_b) - mult("cbk,bq->cqk", part_imag, sin_b)
    spec_imag = mult("cbk,bq->cqk", part_real, sin_b) + mult("cbk,bq->cqk", part_imag, cos_b)
    spec_real, spec_imag = (spec_real, spec_imag)
    filter_real = filter_spectrum[0]
    filter_imag = filter_spectrum[1]
    prod_real = (spec_real * filter_real - spec_imag * filter_imag).astype(jnp.bfloat16)
    prod_imag = (spec_real * filter_imag + spec_imag * filter_real).astype(jnp.bfloat16)
    back_real = mult("cqk,qb->cbk", prod_real, cos_b) + mult("cqk,qb->cbk", prod_imag, sin_b)
    back_imag = mult("cqk,qb->cbk", prod_imag, cos_b) - mult("cqk,qb->cbk", prod_real, sin_b)
    inv_c, inv_s = tables(0, FACTOR_B, ctx_place * freq_cols, freq_cols, points)
    turn_real = (back_real * inv_c + back_imag * inv_s).astype(jnp.bfloat16)
    turn_imag = (back_imag * inv_c - back_real * inv_s).astype(jnp.bfloat16)
    part_real = lax.all_to_all(turn_real, "ctx", split_axis=1, concat_axis=2, tiled=True)
    part_imag = lax.all_to_all(turn_imag, "ctx", split_axis=1, concat_axis=2, tiled=True)
    summed = mult("cbk,ak->cab", part_real, cos_a) + mult("cbk,ak->cab", part_imag, sin_a)
    conv_cols = (summed * inverse_scale).astype(jnp.bfloat16)
    conv_out = lax.all_to_all(conv_cols, "ctx", split_axis=1, concat_axis=2, tiled=True)
    conv_flat = conv_out.reshape(channels, length)
    result = gate_stream * (
        conv_flat.astype(jnp.float32) + gate_bias[:, None] * product.astype(jnp.float32)
    )
    return result.astype(jnp.bfloat16)


def solution(mesh):
    in_specs = (P(None, "ch", "ctx"), P(None, "ch", None), P("ch"), P(None, "ch", None, "ctx"))
    out_specs = P("ch", "ctx")
    return jax.shard_map(
        per_device, mesh=mesh, in_specs=in_specs, out_specs=out_specs, check_vma=False
    )
```

profile of v0, /device:TPU:68, one launch (start us, length us, event | category | flops | bytes accessed | tf_op | source)
XLA Modules:
  0.0 547.2 jit_solution(9452553779208145739)
XLA Ops:
  17.1 16.0 %all-to-all-start = ((bf16[16,2,16384]{2,1,0:T(2,128)(2,1)}), bf16[16,2,16384]{2,1,0:T(2,128)(2,1)S(1)}, u32[]{:S(2)}, u32[]{:S(2)}) async-start(bf16[16,2,16384]{2,1,0:T(2,128)(2,1)} %reshape.139), calls=%async_computation | async-start | bytes 2097152 | tf_op jit(solution)/shard_map/all_to_all | solution.py:61
  34.9 29.7 %all-to-all-done = bf16[16,2,16384]{2,1,0:T(2,128)(2,1)S(1)} async-done(((bf16[16,2,16384]{2,1,0:T(2,128)(2,1)}), bf16[16,2,16384]{2,1,0:T(2,128)(2,1)S(1)}, u32[]{:S(2)}, u32[]{:S(2)}) %all-to-all-start) | async-done | bytes 1048608 | tf_op jit(solution)/shard_map/all_to_all | solution.py:61
  71.9 32.6 %fusion.20 = f32[16,32,2048]{2,1,0:T(8,128)S(1)} fusion(bf16[16,1024,32]{1,2,0:T(8,128)(2,1)S(1)} %all_to_all.75), kind=kOutput, calls=%fused_computation.34 | convolution fusion | flops 2178940928 | bytes 5242880 | tf_op jit(solution)/shard_map/cab,ak->cbk/dot_general | solution.py:38
  104.5 34.5 %add_convert_fusion.1 = (bf16[16,32,2048]{2,1,0:T(8,128)(2,1)}, bf16[16,32,2048]{2,1,0:T(8,128)(2,1)S(1)}) fusion(f32[16,32,2048]{2,1,0:T(8,128)S(1)} %fusion.20, f32[32,2048]{1,0:T(8,128)S(1)} %copy-done.3, f32[32,2048]{1,0:T(8,128)S(1)} %get-tuple-element.16, bf16[16,1024,32]{1,2,0:T(8,128)(2,1)S(1)} %all_to_all.75), kind=kOutput, calls=%fused_computation.29 | convolution fusion | flops 2189426688 | bytes 9961472 | tf_op jit(solution)/shard_map/cab,ak->cbk/dot_general | solution.py:38
  139.1 8.6 %copy.26 = bf16[16,32,2048]{1,0,2:T(8,128)(2,1)} copy(bf16[16,32,2048]{2,1,0:T(8,128)(2,1)S(1)} %get-tuple-element.10) | data formatting | bytes 4194304 | tf_op jit(solution)/shard_map/convert_element_type | solution.py:64
  147.7 14.5 %reshape.141 = bf16[16,2,32768]{2,1,0:T(2,128)(2,1)} reshape(bf16[2048,16,32]{2,1,0:T(8,128)(2,1)} %bitcast.133) | data formatting | bytes 4194304
  165.9 10.0 %copy.28 = bf16[16,32,2048]{1,0,2:T(8,128)(2,1)} copy(bf16[16,32,2048]{2,1,0:T(8,128)(2,1)} %get-tuple-element.9) | data formatting | bytes 4194304 | tf_op jit(solution)/shard_map/convert_element_type | solution.py:65
  175.9 14.5 %reshape.143 = bf16[16,2,32768]{2,1,0:T(2,128)(2,1)} reshape(bf16[2048,16,32]{2,1,0:T(8,128)(2,1)} %bitcast.134) | data formatting | bytes 4194304
  190.4 26.4 %all-to-all-done.1 = bf16[16,2,32768]{2,1,0:T(2,128)(2,1)S(1)} async-done(((bf16[16,2,32768]{2,1,0:T(2,128)(2,1)}), bf16[16,2,32768]{2,1,0:T(2,128)(2,1)S(1)}, u32[]{:S(2)}, u32[]{:S(2)}) %all-to-all-start.1) | async-done | bytes 2097184 | tf_op jit(solution)/shard_map/all_to_all | solution.py:69
  222.7 8.8 %reshape.142 = bf16[2048,16,32]{2,1,0:T(8,128)(2,1)} reshape(bf16[16,2,32768]{2,1,0:T(2,128)(2,1)S(1)} %all-to-all-done.1) | data formatting | bytes 4194304
  231.5 8.5 %copy.27 = bf16[16,32,16,128]{3,1,2,0:T(8,128)(2,1)S(1)} copy(bf16[16,32,16,128]{1,0,3,2:T(8,128)(2,1)} %bitcast.135) | data formatting | bytes 4194304 | tf_op jit(solution)/shard_map/all_to_all | solution.py:69
  252.7 8.9 %all-to-all-done.2 = bf16[16,2,32768]{2,1,0:T(2,128)(2,1)} async-done(((bf16[16,2,32768]{2,1,0:T(2,128)(2,1)}), bf16[16,2,32768]{2,1,0:T(2,128)(2,1)}, u32[]{:S(2)}, u32[]{:S(2)}) %all-to-all-start.2) | async-done | bytes 2097184 | tf_op jit(solution)/shard_map/all_to_all | solution.py:70
  261.6 12.9 %reshape.144 = bf16[2048,16,32]{2,1,0:T(8,128)(2,1)} reshape(bf16[16,2,32768]{2,1,0:T(2,128)(2,1)} %all-to-all-done.2) | data formatting | bytes 4194304
  274.5 8.5 %copy.29 = bf16[16,32,16,128]{3,1,2,0:T(8,128)(2,1)S(1)} copy(bf16[16,32,16,128]{1,0,3,2:T(8,128)(2,1)} %bitcast.136) | data formatting | bytes 4194304 | tf_op jit(solution)/shard_map/all_to_all | solution.py:70
  283.0 6.9 %convolution_subtract_fusion.1 = f32[512,16,128]{2,0,1:T(8,128)S(1)} fusion(f32[512,16,128]{2,0,1:T(8,128)} %fusion.51, bf16[16,512,128]{2,1,0:T(8,128)(2,1)S(1)} %bitcast.138), kind=kOutput, calls=%fused_computation.39 | convolution fusion | flops 1078984704 | bytes 10485760 | tf_op jit(solution)/shard_map/cbk,bq->cqk/dot_general | solution.py:38
  289.9 8.0 %fusion.13 = (bf16[16,512,128]{2,1,0:T(8,128)(2,1)S(1)}, bf16[16,512,128]{2,1,0:T(8,128)(2,1)S(1)}) fusion(f32[512,16,128]{2,0,1:T(8,128)S(1)} %convolution_subtract_fusion.1, f32[2,16,512,128]{3,2,1,0:T(8,128)} %param.7, f32[512,16,128]{2,0,1:T(8,128)S(1)} %copy-done.1, bf16[16,512,128]{2,1,0:T(8,128)(2,1)S(1)} %bitcast.139), kind=kOutput, calls=%fused_computation.24 | convolution fusion | flops 1087111168 | bytes 23068672 | tf_op jit(solution)/shard_map/cbk,bq->cqk/dot_general | solution.py:38
  321.4 7.6 %all-to-all-start.3 = ((bf16[16,512,128]{2,0,1:T(8,128)(2,1)}), bf16[16,512,128]{2,0,1:T(8,128)(2,1)}, u32[]{:S(2)}, u32[]{:S(2)}) async-start(bf16[16,512,128]{2,0,1:T(8,128)(2,1)} %copy.30), calls=%async_computation.3 | async-start | bytes 4194304 | tf_op jit(solution)/shard_map/all_to_all | solution.py:83
  331.6 52.5 %all-to-all-done.3 = bf16[16,512,128]{2,0,1:T(8,128)(2,1)} async-done(((bf16[16,512,128]{2,0,1:T(8,128)(2,1)}), bf16[16,512,128]{2,0,1:T(8,128)(2,1)}, u32[]{:S(2)}, u32[]{:S(2)}) %all-to-all-start.3) | async-done | bytes 2097184 | tf_op jit(solution)/shard_map/all_to_all | solution.py:83
  396.7 24.2 %all-to-all-done.4 = bf16[16,512,128]{2,0,1:T(8,128)(2,1)S(1)} async-done(((bf16[16,512,128]{2,0,1:T(8,128)(2,1)}), bf16[16,512,128]{2,0,1:T(8,128)(2,1)S(1)}, u32[]{:S(2)}, u32[]{:S(2)}) %all-to-all-start.4) | async-done | bytes 2097184 | tf_op jit(solution)/shard_map/all_to_all | solution.py:84
  426.3 32.3 %fusion.14 = f32[1024,16,32]{0,2,1:T(8,128)S(1)} fusion(bf16[16,32,2048]{2,1,0:T(8,128)(2,1)S(1)} %all_to_all.91), kind=kOutput, calls=%fused_computation.31 | convolution fusion | flops 2181038080 | bytes 4194304 | tf_op jit(solution)/shard_map/cbk,ak->cab/dot_general | solution.py:38
  458.7 32.0 %fusion.30 = bf16[16,1024,32]{1,2,0:T(8,128)(2,1)S(1)} fusion(f32[1024,16,32]{0,2,1:T(8,128)S(1)} %fusion.14, bf16[16,32,2048]{2,1,0:T(8,128)(2,1)S(1)} %copy-done.2), kind=kOutput, calls=%fused_computation.55 | convolution fusion | flops 2180513792 | bytes 5242880 | tf_op jit(solution)/shard_map/cbk,ak->cab/dot_general | solution.py:38
  495.5 6.7 %reshape.145 = bf16[16,2,16384]{2,1,0:T(2,128)(2,1)S(1)} reshape(bf16[1024,16,32]{2,1,0:T(8,128)(2,1)} %bitcast.141) | data formatting | bytes 2097152
  502.1 23.2 %all_to_all.99 = bf16[16,2,16384]{2,1,0:T(2,128)(2,1)S(1)} all-to-all(bf16[16,2,16384]{2,1,0:T(2,128)(2,1)S(1)} %reshape.145), channel_id=1, replica_groups=mesh['ctx'=16,'ch'=16] {'ctx'}, dimensions={0} | all-to-all | bytes 2097152 | tf_op jit(solution)/shard_map/all_to_all | solution.py:87
  528.8 7.9 %copy.47 = f32[16,16,64,32]{3,1,2,0:T(8,128)} copy(bf16[16,16,64,32]{3,0,2,1:T(8,128)(2,1)} %bitcast.140) | data formatting | bytes 3145728 | tf_op jit(solution)/shard_map/convert_element_type | solution.py:90
  (48 shorter events, 111.2 us)
Async XLA Ops:
  0.8 2.6 collective-permute-start
  9.6 2.7 copy-start
  17.1 47.6 %all-to-all-start = ((bf16[16,2,16384]{2,1,0:T(2,128)(2,1)}), bf16[16,2,16384]{2,1,0:T(2,128)(2,1)S(1)}, u32[]{:S(2)}, u32[]{:S(2)}) async-start(bf16[16,2,16384]{2,1,0:T(2,128)(2,1)} %reshape.139), calls=%async_computation | async-start | bytes 2097152 | tf_op jit(solution)/shard_map/all_to_all | solution.py:61
  71.9 32.6 %copy-start.3 = (f32[32,2048]{1,0:T(8,128)S(1)}, f32[32,2048]{1,0:T(8,128)}, u32[]{:S(2)}) copy-start(f32[32,2048]{1,0:T(8,128)} %get-tuple-element.17) | copy-start | bytes 786436
  162.1 54.6 %all-to-all-start.1 = ((bf16[16,2,32768]{2,1,0:T(2,128)(2,1)}), bf16[16,2,32768]{2,1,0:T(2,128)(2,1)S(1)}, u32[]{:S(2)}, u32[]{:S(2)}) async-start(bf16[16,2,32768]{2,1,0:T(2,128)(2,1)} %reshape.141), calls=%async_computation.1 | async-start | bytes 4194304 | tf_op jit(solution)/shard_map/all_to_all | solution.py:69
  216.7 44.9 %all-to-all-start.2 = ((bf16[16,2,32768]{2,1,0:T(2,128)(2,1)}), bf16[16,2,32768]{2,1,0:T(2,128)(2,1)}, u32[]{:S(2)}, u32[]{:S(2)}) async-start(bf16[16,2,32768]{2,1,0:T(2,128)(2,1)} %reshape.143), calls=%async_computation.2 | async-start | bytes 4194304 | tf_op jit(solution)/shard_map/all_to_all | solution.py:70
  283.0 6.9 %copy-start.1 = (f32[512,16,128]{2,0,1:T(8,128)S(1)}, f32[512,16,128]{2,0,1:T(8,128)}, u32[]{:S(2)}) copy-start(f32[512,16,128]{2,0,1:T(8,128)} %fusion.43) | copy-start | bytes 12582916
  321.4 62.8 %all-to-all-start.3 = ((bf16[16,512,128]{2,0,1:T(8,128)(2,1)}), bf16[16,512,128]{2,0,1:T(8,128)(2,1)}, u32[]{:S(2)}, u32[]{:S(2)}) async-start(bf16[16,512,128]{2,0,1:T(8,128)(2,1)} %copy.30), calls=%async_computation.3 | async-start | bytes 4194304 | tf_op jit(solution)/shard_map/all_to_all | solution.py:83
  384.1 36.7 %all-to-all-start.4 = ((bf16[16,512,128]{2,0,1:T(8,128)(2,1)}), bf16[16,512,128]{2,0,1:T(8,128)(2,1)S(1)}, u32[]{:S(2)}, u32[]{:S(2)}) async-start(bf16[16,512,128]{2,0,1:T(8,128)(2,1)} %copy.32), calls=%async_computation.4 | async-start | bytes 4194304 | tf_op jit(solution)/shard_map/all_to_all | solution.py:84
  426.3 32.3 %copy-start.2 = (bf16[16,32,2048]{2,1,0:T(8,128)(2,1)S(1)}, bf16[16,32,2048]{2,1,0:T(8,128)(2,1)}, u32[]{:S(2)}) copy-start(bf16[16,32,2048]{2,1,0:T(8,128)(2,1)} %all_to_all.87) | copy-start | bytes 6291460
  536.7 6.0 %copy-start.4 = (f32[16]{0:T(128)S(1)}, f32[16]{0:T(128)}, u32[]{:S(2)}) copy-start(f32[16]{0:T(128)} %param.6) | copy-start | bytes 196
where the time goes:
time: 554 us; the launch traced here: 547 us
  matrix products  180 us (32%)
  local copies, waits for them, and re-layouts  150 us (27%)
  waiting for transfers between devices  142 us (26%)
  starting transfers between devices  38 us (7%)
  blocking collectives  23.2 us (4%)
  other arithmetic  13.6 us (2%)
    dot_general x12, matrix products, mult(): return jnp.einsum(form, left, right, preferred_element_type=jnp.float32)  180 us
    unnamed x21, local copies, waits for them, and re-layouts  67.3 us
    all_to_all x1, waiting for transfers between devices, per_device(): lax.all_to_all(turn_real, 'ctx', split_axis=1, concat_axis=2, tiled=True)  52.5 us
    all_to_all x1, waiting for transfers between devices, per_device(): lax.all_to_all(grid_rows, 'ctx', split_axis=2, concat_axis=1, tiled=True)  29.7 us
    all_to_all x1, waiting for transfers between devices, per_device(): lax.all_to_all(mid_real, 'ctx', split_axis=2, concat_axis=1, tiled=True)  26.4 us
    all_to_all x1, waiting for transfers between devices, per_device(): lax.all_to_all(turn_imag, 'ctx', split_axis=1, concat_axis=2, tiled=True)  24.2 us
    all_to_all x1, blocking collectives, per_device(): lax.all_to_all(conv_cols, 'ctx', split_axis=1, concat_axis=2, tiled=True)  23.2 us
    all_to_all x1, starting transfers between devices, per_device(): lax.all_to_all(grid_rows, 'ctx', split_axis=2, concat_axis=1, tiled=True)  16 us
  transfers between devices with their start and end apart: 6, of which 5 were waited for; matrix products, arithmetic and copies ran while one was open for 12% of the time, Pallas kernels for 0%

commit v1 on v0

v1 whole, which is shorter than its diff:
```python
import math

import jax
import jax.numpy as jnp
import numpy as np
from jax import lax
from jax.experimental import pallas as pl
from jax.experimental.pallas import tpu as pltpu
from jax.sharding import PartitionSpec as P

FACTOR_A = 2048
FACTOR_B = 512
SHORT_TAPS = 3
RING = 4
CHUNKS = (5, 3)
ROWS = 64
KEPT = 128
LANES = 128
COLUMNS = 16384


def send(block, target):
    return lax.ppermute(block, "ctx", [(i, target(i)) for i in range(16)])


def to_core(block):
    return send(block, lambda i: i ^ 1)


def to_far(block):
    return send(block, lambda i: i ^ 2)


def to_next(block):
    return send(block, lambda i: (i + 4) % 16)


def to_last(block):
    return send(block, lambda i: (i - 4) % 16)


def to_across(block):
    return send(block, lambda i: (i + 8) % 16)


def tied(*values):
    return lax.optimization_barrier(values)


def tables(row_index, col_index, size):
    turns = row_index[:, None] * col_index[None, :] % size
    angle = turns.astype(jnp.float32) * (2.0 * math.pi / size)
    return (jnp.cos(angle), -jnp.sin(angle))


def grid_tables():
    index = np.arange(FACTOR_B)
    angle = (index[:, None] * index[None, :] % FACTOR_B) * (2.0 * math.pi / FACTOR_B)
    return jnp.asarray(np.cos(angle), jnp.bfloat16), jnp.asarray(-np.sin(angle), jnp.bfloat16)


def featurize(ref, last_ref, rim_ref, weights):
    last = jnp.where(pl.program_id(0) == 0, rim_ref[0], last_ref[0]).astype(jnp.float32)
    block = ref[0].astype(jnp.float32)
    padded = jnp.concatenate([last, block], axis=1)
    summed = weights[:, 0:1] * block
    for tap in range(1, SHORT_TAPS):
        summed = summed + weights[:, tap : tap + 1] * pltpu.roll(padded, tap, 1)[:, LANES:]
    return summed


def product_kernel(weight_ref, first, first_last, first_rim, third, third_last, third_rim, out):
    left = featurize(first, first_last, first_rim, weight_ref[0].astype(jnp.float32))
    right = featurize(third, third_last, third_rim, weight_ref[2].astype(jnp.float32))
    out[...] = (left * right).astype(jnp.bfloat16)


def gate_kernel(weight_ref, second, second_last, second_rim, out):
    out[...] = featurize(second, second_last, second_rim, weight_ref[1].astype(jnp.float32))


def stream_specs(stream, channels):
    per_step = COLUMNS // LANES
    return [
        pl.BlockSpec((1, channels, COLUMNS), lambda j: (stream, 0, j)),
        pl.BlockSpec((1, channels, LANES), lambda j: (stream, 0, jnp.maximum(j * per_step - 1, 0))),
        pl.BlockSpec((1, channels, LANES), lambda j: (stream, 0, 0)),
    ]


def make_product(weights, streams, rim):
    channels, length = streams.shape[1:]
    return pl.pallas_call(
        product_kernel,
        grid=(length // COLUMNS,),
        in_specs=[pl.BlockSpec(weights.shape, lambda j: (0, 0, 0))]
        + stream_specs(0, channels)
        + stream_specs(2, channels),
        out_specs=pl.BlockSpec((channels, COLUMNS), lambda j: (0, j)),
        out_shape=jax.ShapeDtypeStruct((channels, length), jnp.bfloat16),
        compiler_params=pltpu.CompilerParams(vmem_limit_bytes=56 * 1024 * 1024),
        cost_estimate=pl.CostEstimate(
            flops=14 * channels * length, bytes_accessed=6 * channels * length, transcendentals=0
        ),
    )(weights, streams, streams, rim, streams, streams, rim)


def make_gate(weights, streams, rim):
    channels, length = streams.shape[1:]
    return pl.pallas_call(
        gate_kernel,
        grid=(length // COLUMNS,),
        in_specs=[pl.BlockSpec(weights.shape, lambda j: (0, 0, 0))] + stream_specs(1, channels),
        out_specs=pl.BlockSpec((channels, COLUMNS), lambda j: (0, j)),
        out_shape=jax.ShapeDtypeStruct((channels, length), jnp.float32),
        compiler_params=pltpu.CompilerParams(vmem_limit_bytes=56 * 1024 * 1024),
        cost_estimate=pl.CostEstimate(
            flops=7 * channels * length, bytes_accessed=6 * channels * length, transcendentals=0
        ),
    )(weights, streams, streams, rim)


def dot(left, right):
    return jnp.dot(left, right, preferred_element_type=jnp.float32)


AROUND = (128, 128, 64, 64, 128)
BESIDE = (128, 128, 128, 128)


def conv_kernel(count, core_ref, *refs):
    near, other, fwd_a, inv_a, cos_b, sin_b, cos_ref, sin_ref = refs[count : count + 8]
    half = 2 * KEPT
    block = jnp.concatenate([ref[0] for ref in refs[:count]], axis=0)
    first = dot(fwd_a[...], block)
    cos, sin = cos_ref[...], sin_ref[...]
    real, imag = first[:half], first[half:]
    mid_real = (real * cos - imag * sin).astype(jnp.bfloat16)
    mid_imag = (real * sin + imag * cos).astype(jnp.bfloat16)
    real = dot(mid_real, cos_b[...]) - dot(mid_imag, sin_b[...])
    imag = dot(mid_real, sin_b[...]) + dot(mid_imag, cos_b[...])
    filter_real = jnp.concatenate([near[0, 0].T, other[0, 0].T], axis=0)
    filter_imag = jnp.concatenate([near[1, 0].T, other[1, 0].T], axis=0)
    prod_real = (real * filter_real - imag * filter_imag).astype(jnp.bfloat16)
    prod_imag = (real * filter_imag + imag * filter_real).astype(jnp.bfloat16)
    real = dot(prod_real, cos_b[...]) + dot(prod_imag, sin_b[...])
    imag = dot(prod_imag, cos_b[...]) - dot(prod_real, sin_b[...])
    turn = jnp.concatenate(
        [
            (real * cos + imag * sin).astype(jnp.bfloat16),
            (imag * cos - real * sin).astype(jnp.bfloat16),
        ],
        axis=0,
    )
    scale = 1.0 / (FACTOR_A * FACTOR_B)
    begin = 0
    for out in refs[-count:]:
        rows = out.shape[1]
        out[0] = (dot(inv_a[begin : begin + rows], turn) * scale).astype(jnp.bfloat16)
        begin += rows


def convolve(core, pieces, begin, near, other, shared, around):
    half = near.shape[1] // 2
    channels = pieces[-1].shape[0]
    count = len(pieces)

    def spec(rows, first):
        return pl.BlockSpec((1, rows, FACTOR_B), lambda c, core: (first + c, 0, 0))

    specs = [spec(rows, begin) for rows in AROUND] + [spec(rows, 0) for rows in BESIDE]
    shapes = [(half, rows, FACTOR_B) for rows in AROUND]
    shapes += [(channels, rows, FACTOR_B) for rows in BESIDE]
    spectrum = (2, 1, FACTOR_B, KEPT)
    filters = pl.BlockSpec(spectrum, lambda c, core: (0, core[0] * half + begin + c, 0, 0))
    whole = [pl.BlockSpec(memory_space=pltpu.VMEM) for table in shared]
    inputs = (core, *pieces, near, other, *shared)
    return pl.pallas_call(
        lambda *refs: conv_kernel(count, *refs),
        grid_spec=pltpu.PrefetchScalarGridSpec(
            num_scalar_prefetch=1,
            grid=(channels,),
            in_specs=specs
            + [filters, filters]
            + whole
            + [pl.BlockSpec(memory_space=pl.ANY) for out in around],
            out_specs=specs,
        ),
        out_shape=[jax.ShapeDtypeStruct(shape, jnp.bfloat16) for shape in shapes],
        input_output_aliases={len(inputs) + i: i for i in range(len(around))},
        compiler_params=pltpu.CompilerParams(vmem_limit_bytes=56 * 1024 * 1024),
        cost_estimate=pl.CostEstimate(
            flops=(channels + 1) * 12 * 512 * 512 * 1024,
            bytes_accessed=channels * 3 * 1024 * 1024 + 4 * 1024 * 1024,
            transcendentals=0,
        ),
    )(*inputs, *around)


def gather_ring(far):
    return far, to_last(far), to_across(far), to_next(far)


def scatter_ring(outs):
    own, above, across, below = outs
    return own, to_next(above), to_across(across), to_last(below)


def total(parts):
    summed = joined(parts[0], parts[1])
    for part in parts[2:]:
        summed = summed + part.astype(jnp.float32)
    return summed


def relay(above, below):
    return to_last(above[:, :ROWS]), to_next(below[:, ROWS:])


def joined(block, other):
    return block.astype(jnp.float32) + other.astype(jnp.float32)


def scatter_far(outs):
    _, above, low, high, below = outs
    return to_next(low), to_last(high)


def scatter_near(outs, far):
    own, above, _, _, below = outs
    low = jnp.pad(far[0], ((0, 0), (0, ROWS), (0, 0)))
    high = jnp.pad(far[1], ((0, 0), (ROWS, 0), (0, 0)))
    from_below = to_next(joined(above, low).astype(jnp.bfloat16))
    from_above = to_last(joined(below, high).astype(jnp.bfloat16))
    return joined(own, from_below) + from_above.astype(jnp.float32)


def make_tables(place):
    chip = place // 4
    slot = place % 4
    ring = (chip + jnp.arange(RING, dtype=jnp.int32)) % RING
    here = ring[:, None] * 4 + jnp.stack([slot, slot ^ 1])[None, :]
    there = ring[:, None] * 4 + jnp.stack([slot ^ 2, slot ^ 3])[None, :]
    device = jnp.concatenate([here, there]).reshape(-1)
    row_index = (device[:, None] * ROWS + jnp.arange(ROWS, dtype=jnp.int32)[None, :]).reshape(-1)
    owner = jnp.stack([place, place ^ 1])
    freq_index = (owner[:, None] * KEPT + jnp.arange(KEPT, dtype=jnp.int32)[None, :]).reshape(-1)
    cols = jnp.arange(FACTOR_B, dtype=jnp.int32)
    cos_a, sin_a = tables(freq_index, row_index, FACTOR_A)
    fwd_a = jnp.concatenate([cos_a, sin_a], axis=0).astype(jnp.bfloat16)
    cos_b, sin_b = grid_tables()
    cos_t, sin_t = tables(freq_index, cols, FACTOR_A * FACTOR_B)
    return (fwd_a, fwd_a.T, cos_b, sin_b, cos_t, sin_t)


def per_device(streams, short_weight, gate_bias, filter_spectrum):
    place = lax.axis_index("ctx")
    core = place % 2
    channels = streams.shape[1]
    length = streams.shape[2]
    half = channels // 2
    rim = lax.ppermute(streams[:, :, length - LANES :], "ctx", [(i, i + 1) for i in range(15)])

    product = make_product(short_weight, streams, rim)
    rows = product.reshape(channels, ROWS, FACTOR_B)
    kept = lax.dynamic_slice_in_dim(rows, core * half, half, axis=0)
    passed = to_core(lax.dynamic_slice_in_dim(rows, (1 - core) * half, half, axis=0))
    later, passed, swapped = tied(place, passed, filter_spectrum)
    other = to_core(swapped)
    pair = jnp.concatenate([kept, passed], axis=1)

    which = core[None]
    step = CHUNKS[0]
    ring_pieces = len(AROUND)
    far0 = to_far(pair[:step])
    above_o, below_o = to_last(pair), to_next(pair)
    shared = make_tables(later)
    gate = make_gate(short_weight, streams, rim)
    above_o, below_o, shared, gate = tied(above_o, below_o, shared, gate)
    low_o, high_o = relay(above_o, below_o)
    pieces = gather_ring(far0)
    pair, low_o, high_o = tied(pair, low_o, high_o)
    around = (pair, above_o, low_o, high_o, below_o)
    far1 = to_far(pair[step:])

    *pieces, far1 = tied(*pieces, far1)
    outs0 = convolve(which, (*around, *pieces), 0, filter_spectrum, other, shared, ())
    pieces = gather_ring(far1)
    *pieces, outs0 = tied(*pieces, outs0)
    sum_z0 = total(scatter_ring(outs0[ring_pieces:])).astype(jnp.bfloat16)
    outs1 = convolve(
        which, (*around, *pieces), step, filter_spectrum, other, shared, outs0[:ring_pieces]
    )
    sum_z0, *outs1 = tied(sum_z0, *outs1)
    back0 = to_far(sum_z0)
    sum_z1 = total(scatter_ring(outs1[ring_pieces:])).astype(jnp.bfloat16)
    outs1 = outs1[:ring_pieces]
    low, high, sum_z1, back0 = tied(*scatter_far(outs1), sum_z1, back0)
    back1 = to_far(sum_z1)
    sum_o = scatter_near(outs1, (low, high))
    sums = [
        joined(sum_o[:step], back0).astype(jnp.bfloat16),
        joined(sum_o[step:], back1).astype(jnp.bfloat16),
    ]
    conv = jnp.concatenate(sums, axis=0)
    mine = conv[:, :ROWS]
    swapped = to_core(conv[:, ROWS:])
    conv = jnp.where(
        core == 0, jnp.concatenate([mine, swapped], axis=0), jnp.concatenate([swapped, mine], axis=0)
    )
    conv = conv.reshape(channels, length).astype(jnp.float32)
    direct = gate_bias[:, None] * product.astype(jnp.float32)
    return (gate * (conv + direct)).astype(jnp.bfloat16)


def solution(mesh):
    in_specs = (P(None, "ch", "ctx"), P(None, "ch", None), P("ch"), P(None, "ch", None, "ctx"))
    out_specs = P("ch", "ctx")
    return jax.shard_map(
        per_device, mesh=mesh, in_specs=in_specs, out_specs=out_specs, check_vma=False
    )
```

time: 554 us -> 226 us (0.41); the launches traced: 547 us -> 225 us
  matrix products: 180 us -> 0 us
  local copies, waits for them, and re-layouts: 150 us -> 11.1 us
  Pallas kernels: 0 us -> 41 us
  waiting for transfers between devices: 142 us -> 108 us
  blocking collectives: 23.2 us -> 0 us
  starting transfers between devices: 38 us -> 50.5 us
    dot_general x12 -> x0, matrix products: 180 us -> none  [mult(): return jnp.einsum(form, left, right, preferred_element_type=jnp.float32)]
    all_to_all x5 -> x0, waiting for transfers between devices: 142 us -> none  [the longest x1 52.5 us: per_device(): lax.all_to_all(turn_real, 'ctx', split_axis=1, concat_axis=2, tiled=True)]
    ppermute x1 -> x28, waiting for transfers between devices: 0.01 us -> 108 us  [the longest x27 108 us: send(): return lax.ppermute(block, 'ctx', [(i, target(i)) for i in range(16)])]
    unnamed x21 -> x44, local copies, waits for them, and re-layouts: 67.3 us -> 6.49 us
    ppermute x1 -> x28, starting transfers between devices: 1.73 us -> 50.5 us  [the longest x27 48.8 us: send(): return lax.ppermute(block, 'ctx', [(i, target(i)) for i in range(16)])]
    convert_element_type x8 -> x0, local copies, waits for them, and re-layouts: 44.7 us -> none  [the longest x2 13.9 us: per_device(): conv_flat.astype(jnp.float32)]
    pallas_call x0 -> x4, Pallas kernels: none -> 41 us  [the longest x2 32.2 us: convolve(): pl.pallas_call(lambda *refs: conv_kernel(count, *refs), grid_spec=pltpu.P...]
    all_to_all x8 -> x0, local copies, waits for them, and re-layouts: 36.8 us -> none  [the longest x1 8.46 us: per_device(): lax.all_to_all(mid_real, 'ctx', split_axis=2, concat_axis=1, tiled=True)]
  transfers between devices with their start and end apart: 6 -> 28, of which waited for: 5 -> 18; matrix products, arithmetic and copies ran while one was open for 12% -> 8% of each run, Pallas kernels for 0% -> 16%
where the time goes in v1:
time: 226 us; the launch traced here: 225 us
  waiting for transfers between devices  108 us (48%)
  starting transfers between devices  50.5 us (22%)
  Pallas kernels  41 us (18%)
  other arithmetic  13.9 us (6%)
  local copies, waits for them, and re-layouts  11.1 us (5%)
    ppermute x27, waiting for transfers between devices, send(): return lax.ppermute(block, 'ctx', [(i, target(i)) for i in range(16)])  108 us
    ppermute x27, starting transfers between devices, send(): return lax.ppermute(block, 'ctx', [(i, target(i)) for i in range(16)])  48.8 us
    pallas_call x2, Pallas kernels, convolve(): pl.pallas_call(lambda *refs: conv_kernel(count, *refs), grid_spec=pltpu.P...  32.2 us
    unnamed x44, local copies, waits for them, and re-layouts  6.49 us
    pallas_call x1, Pallas kernels, make_product(): pl.pallas_call(product_kernel, grid=(length // COLUMNS,), in_specs=[pl.Bl...  5.25 us
    another operation x1, other arithmetic  4.71 us
  transfers between devices with their start and end apart: 28, of which 18 were waited for; matrix products, arithmetic and copies ran while one was open for 8% of the time, Pallas kernels for 16%

profile of v1, /device:TPU:68, one launch (start us, length us, event | category | flops | bytes accessed | tf_op | source)
XLA Modules:
  0.0 225.2 jit_solution(6598016422617716800)
XLA Ops:
  4.4 5.2 %shard_map.64 = bf16[16,32768]{1,0:T(8,128)(2,1)} custom-call(bf16[3,16,3]{2,1,0:T(8,128)(2,1)} %copy.20.weight_ref, bf16[3,16,32768]{2,1,0:T(8,128)(2,1)} %second_last.1, bf16[3,16,32768]{2,1,0:T(8,128)(2,1)} %second_last.1, bf16[3,16,128]{2,1,0:T(8,128)(2,1)} %copy-done.8, bf16[3,16,32768]{2,1,0:T(8,128)(2,1)} %second_last.1, ...), custom_call_target="tpu_custom_call" | custom-call | flops 7340032 | bytes 3145728 | tf_op jit(solution)/shard_map/pallas_call | solution.py:93
  11.3 5.8 %collective-permute-start.1 = (bf16[8,64,512]{2,1,0:T(8,128)(2,1)S(1)}, bf16[8,64,512]{2,1,0:T(8,128)(2,1)S(1)}, u32[]{:S(2)}, u32[]{:S(2)}) collective-permute-start(bf16[8,64,512]{2,1,0:T(8,128)(2,1)S(1)} %get-tuple-element.140), channel_id=1, source_target_pairs={{0,16},{16,0},{32,48},{48,32},{64,80},{80,64},{96,112},{112,96},{1... | collective-permute-start | bytes 1572872 | tf_op jit(solution)/shard_map/ppermute | solution.py:23
  19.0 3.5 %shard_map.65 = f32[16,32768]{1,0:T(8,128)} custom-call(bf16[3,16,3]{2,1,0:T(8,128)(2,1)} %copy.20.weight_ref, bf16[3,16,32768]{2,1,0:T(8,128)(2,1)} %second_last.1, bf16[3,16,32768]{2,1,0:T(8,128)(2,1)} %second_last.1, bf16[3,16,128]{2,1,0:T(8,128)(2,1)} %copy-done.8), custom_call_target="tpu_custom_call" | custom-call | flops 3670016 | bytes 3145728 | tf_op jit(solution)/shard_map/pallas_call | solution.py:110
  22.6 4.2 %collective-permute-start.2 = (bf16[8,128,512]{2,1,0:T(8,128)(2,1)S(1)}, bf16[8,128,512]{2,1,0:T(8,128)(2,1)}, u32[]{:S(2)}, u32[]{:S(2)}) collective-permute-start(bf16[8,128,512]{2,1,0:T(8,128)(2,1)S(1)} %pad_maximum_fusion.refs_1_), channel_id=1, source_target_pairs={{0,192},{16,208},{32,224},{48,240},{64,0},{80,16},{96,32},{112,48}... | collective-permute-start | bytes 3145736 | tf_op jit(solution)/shard_map/ppermute | solution.py:23
  27.5 4.5 %collective-permute-start.4 = (bf16[5,128,512]{2,1,0:T(8,128)(2,1)S(1)}, bf16[5,128,512]{2,1,0:T(8,128)(2,1)S(1)}, u32[]{:S(2)}, u32[]{:S(2)}) collective-permute-start(bf16[5,128,512]{2,1,0:T(8,128)(2,1)S(1)} %fusion.5), channel_id=1, source_target_pairs={{0,32},{16,48},{32,0},{48,16},{64,96},{80,112},{96,64},{112,80},{1... | collective-permute-start | bytes 1966088 | tf_op jit(solution)/shard_map/ppermute | solution.py:23
  35.4 4.7 %cosine_convert_fusion = (bf16[256,1024]{0,1:T(8,128)(2,1)S(1)}, bf16[256,1024]{0,1:T(8,128)(2,1)S(1)}) fusion(s32[1024]{0:T(1024)S(1)} %add.172, s32[256]{0:T(256)S(1)} %add_bitcast_fusion), kind=kLoop, calls=%fused_computation.23 | loop fusion | flops 4456448 | bytes 1053696 | tf_op jit(solution)/shard_map/convert
  41.2 8.6 %collective-permute-done.2.refs_2_ = bf16[8,128,512]{2,1,0:T(8,128)(2,1)} collective-permute-done((bf16[8,128,512]{2,1,0:T(8,128)(2,1)S(1)}, bf16[8,128,512]{2,1,0:T(8,128)(2,1)}, u32[]{:S(2)}, u32[]{:S(2)}) %collective-permute-start.2) | collective-permute-done | bytes 1048608 | tf_op jit(solution)/shard_map/ppermute | solution.py:23
  49.8 3.5 %collective-permute-done.3.refs_5_ = bf16[8,128,512]{2,1,0:T(8,128)(2,1)} collective-permute-done((bf16[8,128,512]{2,1,0:T(8,128)(2,1)S(1)}, bf16[8,128,512]{2,1,0:T(8,128)(2,1)}, u32[]{:S(2)}, u32[]{:S(2)}) %collective-permute-start.3) | collective-permute-done | bytes 1048608 | tf_op jit(solution)/shard_map/ppermute | solution.py:23
  57.7 4.4 %collective-permute-done.4.refs_6_ = bf16[5,128,512]{2,1,0:T(8,128)(2,1)S(1)} collective-permute-done((bf16[5,128,512]{2,1,0:T(8,128)(2,1)S(1)}, bf16[5,128,512]{2,1,0:T(8,128)(2,1)S(1)}, u32[]{:S(2)}, u32[]{:S(2)}) %collective-permute-start.4) | collective-permute-done | bytes 655392 | tf_op jit(solution)/shard_map/ppermute | solution.py:23
  65.0 4.3 %collective-permute-done.8.refs_3_ = bf16[8,64,512]{2,1,0:T(8,128)(2,1)S(1)} collective-permute-done((bf16[8,64,512]{2,1,0:T(8,128)(2,1)S(1)}, bf16[8,64,512]{2,1,0:T(8,128)(2,1)S(1)}, u32[]{:S(2)}, u32[]{:S(2)}) %collective-permute-start.8) | collective-permute-done | bytes 524320 | tf_op jit(solution)/shard_map/ppermute | solution.py:23
  69.3 16.3 %collective-permute-done.9.refs_4_ = bf16[8,64,512]{2,1,0:T(8,128)(2,1)} collective-permute-done((bf16[8,64,512]{2,1,0:T(8,128)(2,1)S(1)}, bf16[8,64,512]{2,1,0:T(8,128)(2,1)}, u32[]{:S(2)}, u32[]{:S(2)}) %collective-permute-start.9) | collective-permute-done | bytes 524320 | tf_op jit(solution)/shard_map/ppermute | solution.py:23
  85.7 4.6 %collective-permute-start.10 = (bf16[3,128,512]{2,1,0:T(8,128)(2,1)S(1)}, bf16[3,128,512]{2,1,0:T(8,128)(2,1)S(1)}, u32[]{:S(2)}, u32[]{:S(2)}) collective-permute-start(bf16[3,128,512]{2,1,0:T(8,128)(2,1)S(1)} %slice.31), channel_id=1, source_target_pairs={{0,32},{16,48},{32,0},{48,16},{64,96},{80,112},{96,64},{112,80},{1... | collective-permute-start | bytes 1179656 | tf_op jit(solution)/shard_map/ppermute | solution.py:23
  91.7 6.7 %collective-permute-done.7.refs_9_ = bf16[5,128,512]{2,1,0:T(8,128)(2,1)} collective-permute-done((bf16[5,128,512]{2,1,0:T(8,128)(2,1)S(1)}, bf16[5,128,512]{2,1,0:T(8,128)(2,1)}, u32[]{:S(2)}, u32[]{:S(2)}) %collective-permute-start.7) | collective-permute-done | bytes 655392 | tf_op jit(solution)/shard_map/ppermute | solution.py:23
  103.7 19.2 %shard_map.66 = (bf16[8,128,512]{2,1,0:T(8,128)(2,1)}, bf16[8,128,512]{2,1,0:T(8,128)(2,1)}, bf16[8,64,512]{2,1,0:T(8,128)(2,1)}, bf16[8,64,512]{2,1,0:T(8,128)(...) custom-call(s32[1]{0:T(128)} %bitcast.8.refs_0_, ...), custom_call_target="tpu_custom_call" | custom-call | flops 19327352832 | bytes 19922944 | tf_op jit(solution)/shard_map/pallas_call | solution.py:178
  128.6 13.0 %shard_map.67 = (bf16[8,128,512]{2,1,0:T(8,128)(2,1)}, bf16[8,128,512]{2,1,0:T(8,128)(2,1)}, bf16[8,64,512]{2,1,0:T(8,128)(2,1)}, bf16[8,64,512]{2,1,0:T(8,128)(...) custom-call(s32[1]{0:T(128)} %bitcast.8.refs_0_, ...), custom_call_target="tpu_custom_call", output_to_operand_aliasing={{0}: (18, {}), {1}: (19, {}), {2}: (20, {}), {3}: (21, {}),... | custom-call | flops 12884901888 | bytes 13631488 | tf_op jit(solution)/shard_map/pallas_call | solution.py:178
  141.7 7.7 %collective-permute-done.17 = bf16[5,128,512]{2,1,0:T(8,128)(2,1)S(1)} collective-permute-done((bf16[5,128,512]{2,1,0:T(8,128)(2,1)}, bf16[5,128,512]{2,1,0:T(8,128)(2,1)S(1)}, u32[]{:S(2)}, u32[]{:S(2)}) %collective-permute-start.17) | collective-permute-done | bytes 655392 | tf_op jit(solution)/shard_map/ppermute | solution.py:23
  149.3 3.6 %collective-permute-done.15 = bf16[5,128,512]{2,1,0:T(8,128)(2,1)S(1)} collective-permute-done((bf16[5,128,512]{2,1,0:T(8,128)(2,1)}, bf16[5,128,512]{2,1,0:T(8,128)(2,1)S(1)}, u32[]{:S(2)}, u32[]{:S(2)}) %collective-permute-start.15) | collective-permute-done | bytes 655392 | tf_op jit(solution)/shard_map/ppermute | solution.py:23
  156.3 4.5 %collective-permute-start.23 = (bf16[5,128,512]{2,1,0:T(8,128)(2,1)S(1)}, bf16[5,128,512]{2,1,0:T(8,128)(2,1)S(1)}, u32[]{:S(2)}, u32[]{:S(2)}) collective-permute-start(bf16[5,128,512]{2,1,0:T(8,128)(2,1)S(1)} %add_convert_fusion.2), channel_id=1, source_target_pairs={{0,32},{16,48},{32,0},{48,16},{64,96},{80,112},{96,64},{112,80},{1... | collective-permute-start | bytes 1966088 | tf_op jit(solution)/shard_map/ppermute | solution.py:23
  161.9 3.6 %collective-permute-done.22 = bf16[3,128,512]{2,1,0:T(8,128)(2,1)S(1)} collective-permute-done((bf16[3,128,512]{2,1,0:T(8,128)(2,1)}, bf16[3,128,512]{2,1,0:T(8,128)(2,1)S(1)}, u32[]{:S(2)}, u32[]{:S(2)}) %collective-permute-start.22) | collective-permute-done | bytes 393248 | tf_op jit(solution)/shard_map/ppermute | solution.py:23
  167.6 7.0 %collective-permute-done.20 = bf16[3,128,512]{2,1,0:T(8,128)(2,1)S(1)} collective-permute-done((bf16[3,128,512]{2,1,0:T(8,128)(2,1)S(1)}, bf16[3,128,512]{2,1,0:T(8,128)(2,1)S(1)}, u32[]{:S(2)}, u32[]{:S(2)}) %collective-permute-start.20) | collective-permute-done | bytes 393248 | tf_op jit(solution)/shard_map/ppermute | solution.py:23
  174.7 10.9 %collective-permute-done.18 = bf16[8,64,512]{2,1,0:T(8,128)(2,1)S(1)} collective-permute-done((bf16[8,64,512]{2,1,0:T(8,128)(2,1)S(1)}, bf16[8,64,512]{2,1,0:T(8,128)(2,1)S(1)}, u32[]{:S(2)}, u32[]{:S(2)}) %collective-permute-start.18) | collective-permute-done | bytes 524320 | tf_op jit(solution)/shard_map/ppermute | solution.py:23
  185.7 3.9 %collective-permute-done.23 = bf16[5,128,512]{2,1,0:T(8,128)(2,1)S(1)} collective-permute-done((bf16[5,128,512]{2,1,0:T(8,128)(2,1)S(1)}, bf16[5,128,512]{2,1,0:T(8,128)(2,1)S(1)}, u32[]{:S(2)}, u32[]{:S(2)}) %collective-permute-start.23) | collective-permute-done | bytes 655392 | tf_op jit(solution)/shard_map/ppermute | solution.py:23
  192.3 4.9 %collective-permute-start.26 = (bf16[3,128,512]{2,1,0:T(8,128)(2,1)S(1)}, bf16[3,128,512]{2,1,0:T(8,128)(2,1)S(1)}, u32[]{:S(2)}, u32[]{:S(2)}) collective-permute-start(bf16[3,128,512]{2,1,0:T(8,128)(2,1)S(1)} %add_convert_fusion.3), channel_id=1, source_target_pairs={{0,32},{16,48},{32,0},{48,16},{64,96},{80,112},{96,64},{112,80},{1... | collective-permute-start | bytes 1179656 | tf_op jit(solution)/shard_map/ppermute | solution.py:23
  197.2 17.5 %collective-permute-done.25 = bf16[8,128,512]{2,1,0:T(8,128)(2,1)S(1)} collective-permute-done((bf16[8,128,512]{2,1,0:T(8,128)(2,1)S(1)}, bf16[8,128,512]{2,1,0:T(8,128)(2,1)S(1)}, u32[]{:S(2)}, u32[]{:S(2)}) %collective-permute-start.25) | collective-permute-done | bytes 1048608 | tf_op jit(solution)/shard_map/ppermute | solution.py:23
  (110 shorter events, 52.6 us)
Async XLA Ops:
  18.6 85.0 %collective-permute-start.14 = (f32[2,16,512,128]{3,2,1,0:T(8,128)}, f32[2,16,512,128]{3,2,1,0:T(8,128)}, u32[]{:S(2)}, u32[]{:S(2)}) collective-permute-start(f32[2,16,512,128]{3,2,1,0:T(8,128)} %refs_10_.3), channel_id=1, source_target_pairs={{0,16},{16,0},{32,48},{48,32},{64,80},{80,64},{96,112},{112,96},{1... | collective-permute-start | bytes 25165832 | tf_op jit(solution)/shard_map/ppermute | solution.py:23
  22.6 27.2 %collective-permute-start.2 = (bf16[8,128,512]{2,1,0:T(8,128)(2,1)S(1)}, bf16[8,128,512]{2,1,0:T(8,128)(2,1)}, u32[]{:S(2)}, u32[]{:S(2)}) collective-permute-start(bf16[8,128,512]{2,1,0:T(8,128)(2,1)S(1)} %pad_maximum_fusion.refs_1_), channel_id=1, source_target_pairs={{0,192},{16,208},{32,224},{48,240},{64,0},{80,16},{96,32},{112,48}... | collective-permute-start | bytes 3145736 | tf_op jit(solution)/shard_map/ppermute | solution.py:23
  26.9 26.5 %collective-permute-start.3 = (bf16[8,128,512]{2,1,0:T(8,128)(2,1)S(1)}, bf16[8,128,512]{2,1,0:T(8,128)(2,1)}, u32[]{:S(2)}, u32[]{:S(2)}) collective-permute-start(bf16[8,128,512]{2,1,0:T(8,128)(2,1)S(1)} %pad_maximum_fusion.refs_1_), channel_id=1, source_target_pairs={{0,64},{16,80},{32,96},{48,112},{64,128},{80,144},{96,160},{112,17... | collective-permute-start | bytes 3145736 | tf_op jit(solution)/shard_map/ppermute | solution.py:23
  27.5 34.6 %collective-permute-start.4 = (bf16[5,128,512]{2,1,0:T(8,128)(2,1)S(1)}, bf16[5,128,512]{2,1,0:T(8,128)(2,1)S(1)}, u32[]{:S(2)}, u32[]{:S(2)}) collective-permute-start(bf16[5,128,512]{2,1,0:T(8,128)(2,1)S(1)} %fusion.5), channel_id=1, source_target_pairs={{0,32},{16,48},{32,0},{48,16},{64,96},{80,112},{96,64},{112,80},{1... | collective-permute-start | bytes 1966088 | tf_op jit(solution)/shard_map/ppermute | solution.py:23
  54.4 14.9 %collective-permute-start.8 = (bf16[8,64,512]{2,1,0:T(8,128)(2,1)S(1)}, bf16[8,64,512]{2,1,0:T(8,128)(2,1)S(1)}, u32[]{:S(2)}, u32[]{:S(2)}) collective-permute-start(bf16[8,64,512]{2,1,0:T(8,128)(2,1)S(1)} %slice.29), channel_id=1, source_target_pairs={{0,192},{16,208},{32,224},{48,240},{64,0},{80,16},{96,32},{112,48}... | collective-permute-start | bytes 1572872 | tf_op jit(solution)/shard_map/ppermute | solution.py:23
  55.8 29.8 %collective-permute-start.9 = (bf16[8,64,512]{2,1,0:T(8,128)(2,1)S(1)}, bf16[8,64,512]{2,1,0:T(8,128)(2,1)}, u32[]{:S(2)}, u32[]{:S(2)}) collective-permute-start(bf16[8,64,512]{2,1,0:T(8,128)(2,1)S(1)} %slice.30), channel_id=1, source_target_pairs={{0,64},{16,80},{32,96},{48,112},{64,128},{80,144},{96,160},{112,17... | collective-permute-start | bytes 1572872 | tf_op jit(solution)/shard_map/ppermute | solution.py:23
  62.1 29.6 %collective-permute-start.5 = (bf16[5,128,512]{2,1,0:T(8,128)(2,1)S(1)}, bf16[5,128,512]{2,1,0:T(8,128)(2,1)}, u32[]{:S(2)}, u32[]{:S(2)}) collective-permute-start(bf16[5,128,512]{2,1,0:T(8,128)(2,1)S(1)} %collective-permute-done.4.refs_6_), channel_id=1, source_target_pairs={{0,192},{16,208},{32,224},{48,240},{64,0},{80,16},{96,32},{112,48}... | collective-permute-start | bytes 1966088 | tf_op jit(solution)/shard_map/ppermute | solution.py:23
  65.0 26.7 %collective-permute-start.6 = (bf16[5,128,512]{2,1,0:T(8,128)(2,1)S(1)}, bf16[5,128,512]{2,1,0:T(8,128)(2,1)}, u32[]{:S(2)}, u32[]{:S(2)}) collective-permute-start(bf16[5,128,512]{2,1,0:T(8,128)(2,1)S(1)} %collective-permute-done.4.refs_6_), channel_id=1, source_target_pairs={{0,128},{16,144},{32,160},{48,176},{64,192},{80,208},{96,224},{112... | collective-permute-start | bytes 1966088 | tf_op jit(solution)/shard_map/ppermute | solution.py:23
  69.3 29.1 %collective-permute-start.7 = (bf16[5,128,512]{2,1,0:T(8,128)(2,1)S(1)}, bf16[5,128,512]{2,1,0:T(8,128)(2,1)}, u32[]{:S(2)}, u32[]{:S(2)}) collective-permute-start(bf16[5,128,512]{2,1,0:T(8,128)(2,1)S(1)} %collective-permute-done.4.refs_6_), channel_id=1, source_target_pairs={{0,64},{16,80},{32,96},{48,112},{64,128},{80,144},{96,160},{112,17... | collective-permute-start | bytes 1966088 | tf_op jit(solution)/shard_map/ppermute | solution.py:23
  85.7 15.9 %collective-permute-start.10 = (bf16[3,128,512]{2,1,0:T(8,128)(2,1)S(1)}, bf16[3,128,512]{2,1,0:T(8,128)(2,1)S(1)}, u32[]{:S(2)}, u32[]{:S(2)}) collective-permute-start(bf16[3,128,512]{2,1,0:T(8,128)(2,1)S(1)} %slice.31), channel_id=1, source_target_pairs={{0,32},{16,48},{32,0},{48,16},{64,96},{80,112},{96,64},{112,80},{1... | collective-permute-start | bytes 1179656 | tf_op jit(solution)/shard_map/ppermute | solution.py:23
  101.6 21.2 %collective-permute-start.11 = (bf16[3,128,512]{2,1,0:T(8,128)(2,1)S(1)}, bf16[3,128,512]{2,1,0:T(8,128)(2,1)S(1)}, u32[]{:S(2)}, u32[]{:S(2)}) collective-permute-start(bf16[3,128,512]{2,1,0:T(8,128)(2,1)S(1)} %collective-permute-done.10.refs_6_), channel_id=1, source_target_pairs={{0,192},{16,208},{32,224},{48,240},{64,0},{80,16},{96,32},{112,48}... | collective-permute-start | bytes 1179656 | tf_op jit(solution)/shard_map/ppermute | solution.py:23
  101.6 21.2 %collective-permute-start.12 = (bf16[3,128,512]{2,1,0:T(8,128)(2,1)S(1)}, bf16[3,128,512]{2,1,0:T(8,128)(2,1)S(1)}, u32[]{:S(2)}, u32[]{:S(2)}) collective-permute-start(bf16[3,128,512]{2,1,0:T(8,128)(2,1)S(1)} %collective-permute-done.10.refs_6_), channel_id=1, source_target_pairs={{0,128},{16,144},{32,160},{48,176},{64,192},{80,208},{96,224},{112... | collective-permute-start | bytes 1179656 | tf_op jit(solution)/shard_map/ppermute | solution.py:23
  101.6 21.3 %collective-permute-start.13 = (bf16[3,128,512]{2,1,0:T(8,128)(2,1)S(1)}, bf16[3,128,512]{2,1,0:T(8,128)(2,1)S(1)}, u32[]{:S(2)}, u32[]{:S(2)}) collective-permute-start(bf16[3,128,512]{2,1,0:T(8,128)(2,1)S(1)} %collective-permute-done.10.refs_6_), channel_id=1, source_target_pairs={{0,64},{16,80},{32,96},{48,112},{64,128},{80,144},{96,160},{112,17... | collective-permute-start | bytes 1179656 | tf_op jit(solution)/shard_map/ppermute | solution.py:23
  122.9 26.4 %collective-permute-start.17 = (bf16[5,128,512]{2,1,0:T(8,128)(2,1)}, bf16[5,128,512]{2,1,0:T(8,128)(2,1)S(1)}, u32[]{:S(2)}, u32[]{:S(2)}) collective-permute-start(bf16[5,128,512]{2,1,0:T(8,128)(2,1)} %get-tuple-element.102), channel_id=1, source_target_pairs={{0,192},{16,208},{32,224},{48,240},{64,0},{80,16},{96,32},{112,48}... | collective-permute-start | bytes 1966088 | tf_op jit(solution)/shard_map/ppermute | solution.py:23
  125.7 23.6 %collective-permute-start.16 = (bf16[5,128,512]{2,1,0:T(8,128)(2,1)}, bf16[5,128,512]{2,1,0:T(8,128)(2,1)S(1)}, u32[]{:S(2)}, u32[]{:S(2)}) collective-permute-start(bf16[5,128,512]{2,1,0:T(8,128)(2,1)} %get-tuple-element.101), channel_id=1, source_target_pairs={{0,128},{16,144},{32,160},{48,176},{64,192},{80,208},{96,224},{112... | collective-permute-start | bytes 1966088 | tf_op jit(solution)/shard_map/ppermute | solution.py:23
  127.3 25.6 %collective-permute-start.15 = (bf16[5,128,512]{2,1,0:T(8,128)(2,1)}, bf16[5,128,512]{2,1,0:T(8,128)(2,1)S(1)}, u32[]{:S(2)}, u32[]{:S(2)}) collective-permute-start(bf16[5,128,512]{2,1,0:T(8,128)(2,1)} %get-tuple-element.100), channel_id=1, source_target_pairs={{0,64},{16,80},{32,96},{48,112},{64,128},{80,144},{96,160},{112,17... | collective-permute-start | bytes 1966088 | tf_op jit(solution)/shard_map/ppermute | solution.py:23
  154.0 13.6 %collective-permute-start.21 = (bf16[3,128,512]{2,1,0:T(8,128)(2,1)S(1)}, bf16[3,128,512]{2,1,0:T(8,128)(2,1)S(1)}, u32[]{:S(2)}, u32[]{:S(2)}) collective-permute-start(bf16[3,128,512]{2,1,0:T(8,128)(2,1)S(1)} %copy-done.16), channel_id=1, source_target_pairs={{0,128},{16,144},{32,160},{48,176},{64,192},{80,208},{96,224},{112... | collective-permute-start | bytes 1179656 | tf_op jit(solution)/shard_map/ppermute | solution.py:23
  155.5 19.0 %collective-permute-start.20 = (bf16[3,128,512]{2,1,0:T(8,128)(2,1)S(1)}, bf16[3,128,512]{2,1,0:T(8,128)(2,1)S(1)}, u32[]{:S(2)}, u32[]{:S(2)}) collective-permute-start(bf16[3,128,512]{2,1,0:T(8,128)(2,1)S(1)} %copy-done.15), channel_id=1, source_target_pairs={{0,64},{16,80},{32,96},{48,112},{64,128},{80,144},{96,160},{112,17... | collective-permute-start | bytes 1179656 | tf_op jit(solution)/shard_map/ppermute | solution.py:23
  156.3 33.3 %collective-permute-start.23 = (bf16[5,128,512]{2,1,0:T(8,128)(2,1)S(1)}, bf16[5,128,512]{2,1,0:T(8,128)(2,1)S(1)}, u32[]{:S(2)}, u32[]{:S(2)}) collective-permute-start(bf16[5,128,512]{2,1,0:T(8,128)(2,1)S(1)} %add_convert_fusion.2), channel_id=1, source_target_pairs={{0,32},{16,48},{32,0},{48,16},{64,96},{80,112},{96,64},{112,80},{1... | collective-permute-start | bytes 1966088 | tf_op jit(solution)/shard_map/ppermute | solution.py:23
  160.8 24.9 %collective-permute-start.18 = (bf16[8,64,512]{2,1,0:T(8,128)(2,1)S(1)}, bf16[8,64,512]{2,1,0:T(8,128)(2,1)S(1)}, u32[]{:S(2)}, u32[]{:S(2)}) collective-permute-start(bf16[8,64,512]{2,1,0:T(8,128)(2,1)S(1)} %copy-done.12), channel_id=1, source_target_pairs={{0,64},{16,80},{32,96},{48,112},{64,128},{80,144},{96,160},{112,17... | collective-permute-start | bytes 1572872 | tf_op jit(solution)/shard_map/ppermute | solution.py:23
  165.5 20.1 %collective-permute-start.19 = (bf16[8,64,512]{2,1,0:T(8,128)(2,1)S(1)}, bf16[8,64,512]{2,1,0:T(8,128)(2,1)S(1)}, u32[]{:S(2)}, u32[]{:S(2)}) collective-permute-start(bf16[8,64,512]{2,1,0:T(8,128)(2,1)S(1)} %copy-done.13), channel_id=1, source_target_pairs={{0,192},{16,208},{32,224},{48,240},{64,0},{80,16},{96,32},{112,48}... | collective-permute-start | bytes 1572872 | tf_op jit(solution)/shard_map/ppermute | solution.py:23
  189.8 25.0 %collective-permute-start.25 = (bf16[8,128,512]{2,1,0:T(8,128)(2,1)S(1)}, bf16[8,128,512]{2,1,0:T(8,128)(2,1)S(1)}, u32[]{:S(2)}, u32[]{:S(2)}) collective-permute-start(bf16[8,128,512]{2,1,0:T(8,128)(2,1)S(1)} %add_convert_fusion), channel_id=1, source_target_pairs={{0,192},{16,208},{32,224},{48,240},{64,0},{80,16},{96,32},{112,48}... | collective-permute-start | bytes 3145736 | tf_op jit(solution)/shard_map/ppermute | solution.py:23
  192.2 25.9 %collective-permute-start.24 = (bf16[8,128,512]{2,1,0:T(8,128)(2,1)S(1)}, bf16[8,128,512]{2,1,0:T(8,128)(2,1)S(1)}, u32[]{:S(2)}, u32[]{:S(2)}) collective-permute-start(bf16[8,128,512]{2,1,0:T(8,128)(2,1)S(1)} %add_convert_fusion.1), channel_id=1, source_target_pairs={{0,64},{16,80},{32,96},{48,112},{64,128},{80,144},{96,160},{112,17... | collective-permute-start | bytes 3145736 | tf_op jit(solution)/shard_map/ppermute | solution.py:23
  192.3 26.5 %collective-permute-start.26 = (bf16[3,128,512]{2,1,0:T(8,128)(2,1)S(1)}, bf16[3,128,512]{2,1,0:T(8,128)(2,1)S(1)}, u32[]{:S(2)}, u32[]{:S(2)}) collective-permute-start(bf16[3,128,512]{2,1,0:T(8,128)(2,1)S(1)} %add_convert_fusion.3), channel_id=1, source_target_pairs={{0,32},{16,48},{32,0},{48,16},{64,96},{80,112},{96,64},{112,80},{1... | collective-permute-start | bytes 1179656 | tf_op jit(solution)/shard_map/ppermute | solution.py:23
  (24 other events, 461.4 us)

commit v2 on v1

--- a/solution.py
+++ b/solution.py
@@ -12,7 +12,7 @@
 FACTOR_B = 512
 SHORT_TAPS = 3
 RING = 4
-CHUNKS = (5, 3)
+CHUNKS = (4, 4)
 ROWS = 64
 KEPT = 128
 LANES = 128
@@ -275,15 +275,15 @@
     far0 = to_far(pair[:step])
     above_o, below_o = to_last(pair), to_next(pair)
     shared = make_tables(later)
+    above_o, below_o, shared = tied(above_o, below_o, shared)
+    low_o, high_o = relay(above_o, below_o)
+    far0, rim, pair = tied(far0, rim, pair)
+    pieces = gather_ring(far0)
     gate = make_gate(short_weight, streams, rim)
-    above_o, below_o, shared, gate = tied(above_o, below_o, shared, gate)
-    low_o, high_o = relay(above_o, below_o)
-    pieces = gather_ring(far0)
-    pair, low_o, high_o = tied(pair, low_o, high_o)
     around = (pair, above_o, low_o, high_o, below_o)
     far1 = to_far(pair[step:])
 
-    *pieces, far1 = tied(*pieces, far1)
+    *pieces, far1, gate = tied(*pieces, far1, gate)
     outs0 = convolve(which, (*around, *pieces), 0, filter_spectrum, other, shared, ())
     pieces = gather_ring(far1)
     *pieces, outs0 = tied(*pieces, outs0)

time: 226 us -> 220 us (0.973)
  the two profiles are of different devices: /device:TPU:68 before, /device:TPU:103 now
where the time goes in v2:
time: 220 us; the launch traced here: 219 us
  waiting for transfers between devices  105 us (48%)
  starting transfers between devices  48.4 us (22%)
  Pallas kernels  41 us (19%)
  other arithmetic  13.9 us (6%)
  local copies, waits for them, and re-layouts  10.8 us (5%)
    ppermute x27, waiting for transfers between devices, send(): return lax.ppermute(block, 'ctx', [(i, target(i)) for i in range(16)])  105 us
    ppermute x27, starting transfers between devices, send(): return lax.ppermute(block, 'ctx', [(i, target(i)) for i in range(16)])  41.7 us
    pallas_call x2, Pallas kernels, convolve(): pl.pallas_call(lambda *refs: conv_kernel(count, *refs), grid_spec=pltpu.P...  32.2 us
    ppermute x1, starting transfers between devices, per_device(): lax.ppermute(streams[:, :, length - LANES:], 'ctx', [(i, i + 1) for i in...  6.67 us
    unnamed x42, local copies, waits for them, and re-layouts  6.25 us
    pallas_call x1, Pallas kernels, make_product(): pl.pallas_call(product_kernel, grid=(length // COLUMNS,), in_specs=[pl.Bl...  5.25 us
    another operation x1, other arithmetic  4.71 us
  transfers between devices with their start and end apart: 28, of which 13 were waited for; matrix products, arithmetic and copies ran while one was open for 8% of the time, Pallas kernels for 16%

profile of v2, /device:TPU:103, one launch (start us, length us, event | category | flops | bytes accessed | tf_op | source)
XLA Modules:
  0.0 219.1 jit_solution(8320765022162648520)
XLA Ops:
  0.7 6.7 %collective-permute-start = (bf16[3,16,128]{2,1,0:T(8,128)(2,1)S(1)}, bf16[3,16,128]{2,1,0:T(8,128)(2,1)S(1)}, u32[]{:S(2)}, u32[]{:S(2)}) collective-permute-start(bf16[3,16,128]{2,1,0:T(8,128)(2,1)S(1)} %slice.27), channel_id=1, source_target_pairs={{0,16},{16,32},{32,48},{48,64},{64,80},{80,96},{96,112},{112,128},... | collective-permute-start | bytes 36872 | tf_op jit(solution)/shard_map/ppermute | solution.py:262
  9.4 5.2 %shard_map.64 = bf16[16,32768]{1,0:T(8,128)(2,1)} custom-call(bf16[3,16,3]{2,1,0:T(8,128)(2,1)} %copy.20.weight_ref, bf16[3,16,32768]{2,1,0:T(8,128)(2,1)} %second_last.1, bf16[3,16,32768]{2,1,0:T(8,128)(2,1)} %second_last.1, bf16[3,16,128]{2,1,0:T(8,128)(2,1)} %copy-done.8, bf16[3,16,32768]{2,1,0:T(8,128)(2,1)} %second_last.1, ...), custom_call_target="tpu_custom_call" | custom-call | flops 7340032 | bytes 3145728 | tf_op jit(solution)/shard_map/pallas_call | solution.py:93
  16.4 1.9 collective-permute-done.1
  18.5 5.1 %collective-permute-start.10 = (bf16[8,128,512]{2,1,0:T(8,128)(2,1)S(1)}, bf16[8,128,512]{2,1,0:T(8,128)(2,1)}, u32[]{:S(2)}, u32[]{:S(2)}) collective-permute-start(bf16[8,128,512]{2,1,0:T(8,128)(2,1)S(1)} %pad_maximum_fusion.refs_1_), channel_id=1, source_target_pairs={{0,192},{16,208},{32,224},{48,240},{64,0},{80,16},{96,32},{112,48}... | collective-permute-start | bytes 3145736 | tf_op jit(solution)/shard_map/ppermute | solution.py:23
  23.6 3.4 %collective-permute-start.2 = (bf16[4,128,512]{2,1,0:T(8,128)(2,1)S(1)}, bf16[4,128,512]{2,1,0:T(8,128)(2,1)S(1)}, u32[]{:S(2)}, u32[]{:S(2)}) collective-permute-start(bf16[4,128,512]{2,1,0:T(8,128)(2,1)S(1)} %fusion.10), channel_id=1, source_target_pairs={{0,32},{16,48},{32,0},{48,16},{64,96},{80,112},{96,64},{112,80},{1... | collective-permute-start | bytes 1572872 | tf_op jit(solution)/shard_map/ppermute | solution.py:23
  27.7 24.3 %collective-permute-done.2.refs_6_ = bf16[4,128,512]{2,1,0:T(8,128)(2,1)S(1)} collective-permute-done((bf16[4,128,512]{2,1,0:T(8,128)(2,1)S(1)}, bf16[4,128,512]{2,1,0:T(8,128)(2,1)S(1)}, u32[]{:S(2)}, u32[]{:S(2)}) %collective-permute-start.2) | collective-permute-done | bytes 524320 | tf_op jit(solution)/shard_map/ppermute | solution.py:23
  52.0 2.4 %collective-permute-start.3 = (bf16[4,128,512]{2,1,0:T(8,128)(2,1)S(1)}, bf16[4,128,512]{2,1,0:T(8,128)(2,1)S(1)}, u32[]{:S(2)}, u32[]{:S(2)}) collective-permute-start(bf16[4,128,512]{2,1,0:T(8,128)(2,1)S(1)} %collective-permute-done.2.refs_6_), channel_id=1, source_target_pairs={{0,192},{16,208},{32,224},{48,240},{64,0},{80,16},{96,32},{112,48}... | collective-permute-start | bytes 1572872 | tf_op jit(solution)/shard_map/ppermute | solution.py:23
  54.3 4.7 %cosine_convert_fusion = (bf16[256,1024]{0,1:T(8,128)(2,1)S(1)}, bf16[256,1024]{0,1:T(8,128)(2,1)S(1)}) fusion(s32[1024]{0:T(1024)S(1)} %add.172, s32[256]{0:T(256)S(1)} %add_bitcast_fusion), kind=kLoop, calls=%fused_computation.26 | loop fusion | flops 4456448 | bytes 1053696 | tf_op jit(solution)/shard_map/convert
  60.2 3.2 %sine_negate_fusion = (f32[256,512]{1,0:T(8,128)}, f32[256,512]{1,0:T(8,128)}) fusion(s32[256]{0:T(256)S(1)} %add_bitcast_fusion), kind=kLoop, calls=%fused_computation.37 | loop fusion | flops 1966080 | bytes 1049600 | tf_op jit(solution)/shard_map/neg | solution.py:53
  64.1 3.5 %collective-permute-start.6 = (bf16[4,128,512]{2,1,0:T(8,128)(2,1)S(1)}, bf16[4,128,512]{2,1,0:T(8,128)(2,1)S(1)}, u32[]{:S(2)}, u32[]{:S(2)}) collective-permute-start(bf16[4,128,512]{2,1,0:T(8,128)(2,1)S(1)} %slice.29), channel_id=1, source_target_pairs={{0,32},{16,48},{32,0},{48,16},{64,96},{80,112},{96,64},{112,80},{1... | collective-permute-start | bytes 1572872 | tf_op jit(solution)/shard_map/ppermute | solution.py:23
  69.9 2.2 collective-permute-start.12
  72.0 4.8 %collective-permute-start.13 = (bf16[8,64,512]{2,1,0:T(8,128)(2,1)S(1)}, bf16[8,64,512]{2,1,0:T(8,128)(2,1)}, u32[]{:S(2)}, u32[]{:S(2)}) collective-permute-start(bf16[8,64,512]{2,1,0:T(8,128)(2,1)S(1)} %slice.31), channel_id=1, source_target_pairs={{0,64},{16,80},{32,96},{48,112},{64,128},{80,144},{96,160},{112,17... | collective-permute-start | bytes 1572872 | tf_op jit(solution)/shard_map/ppermute | solution.py:23
  76.8 3.5 %shard_map.65 = f32[16,32768]{1,0:T(8,128)} custom-call(bf16[3,16,3]{2,1,0:T(8,128)(2,1)} %copy.20.weight_ref, bf16[3,16,32768]{2,1,0:T(8,128)(2,1)} %second_last.1, bf16[3,16,32768]{2,1,0:T(8,128)(2,1)} %second_last.1, bf16[3,16,128]{2,1,0:T(8,128)(2,1)} %copy-done.8), custom_call_target="tpu_custom_call" | custom-call | flops 3670016 | bytes 3145728 | tf_op jit(solution)/shard_map/pallas_call | solution.py:110
  80.4 10.6 %collective-permute-done.6.refs_6_ = bf16[4,128,512]{2,1,0:T(8,128)(2,1)S(1)} collective-permute-done((bf16[4,128,512]{2,1,0:T(8,128)(2,1)S(1)}, bf16[4,128,512]{2,1,0:T(8,128)(2,1)S(1)}, u32[]{:S(2)}, u32[]{:S(2)}) %collective-permute-start.6) | collective-permute-done | bytes 524320 | tf_op jit(solution)/shard_map/ppermute | solution.py:23
  90.9 2.1 collective-permute-start.7
  96.1 16.1 %shard_map.66 = (bf16[8,128,512]{2,1,0:T(8,128)(2,1)}, bf16[8,128,512]{2,1,0:T(8,128)(2,1)}, bf16[8,64,512]{2,1,0:T(8,128)(2,1)}, bf16[8,64,512]{2,1,0:T(8,128)(...) custom-call(s32[1]{0:T(128)} %bitcast.refs_0_, ...), custom_call_target="tpu_custom_call" | custom-call | flops 16106127360 | bytes 16777216 | tf_op jit(solution)/shard_map/pallas_call | solution.py:178
  112.3 7.4 %collective-permute-done.9.refs_9_ = bf16[4,128,512]{2,1,0:T(8,128)(2,1)S(1)} collective-permute-done((bf16[4,128,512]{2,1,0:T(8,128)(2,1)S(1)}, bf16[4,128,512]{2,1,0:T(8,128)(2,1)S(1)}, u32[]{:S(2)}, u32[]{:S(2)}) %collective-permute-start.9) | collective-permute-done | bytes 524320 | tf_op jit(solution)/shard_map/ppermute | solution.py:23
  122.3 16.1 %shard_map.67 = (bf16[8,128,512]{2,1,0:T(8,128)(2,1)}, bf16[8,128,512]{2,1,0:T(8,128)(2,1)}, bf16[8,64,512]{2,1,0:T(8,128)(2,1)}, bf16[8,64,512]{2,1,0:T(8,128)(...) custom-call(s32[1]{0:T(128)} %bitcast.refs_0_, ...), custom_call_target="tpu_custom_call", output_to_operand_aliasing={{0}: (18, {}), {1}: (19, {}), {2}: (20, {}), {3}: (21, {}),... | custom-call | flops 16106127360 | bytes 16777216 | tf_op jit(solution)/shard_map/pallas_call | solution.py:178
  138.4 8.1 %collective-permute-done.15 = bf16[4,128,512]{2,1,0:T(8,128)(2,1)S(1)} collective-permute-done((bf16[4,128,512]{2,1,0:T(8,128)(2,1)}, bf16[4,128,512]{2,1,0:T(8,128)(2,1)S(1)}, u32[]{:S(2)}, u32[]{:S(2)}) %collective-permute-start.15) | collective-permute-done | bytes 524320 | tf_op jit(solution)/shard_map/ppermute | solution.py:23
  151.5 8.6 %collective-permute-done.22 = bf16[4,128,512]{2,1,0:T(8,128)(2,1)S(1)} collective-permute-done((bf16[4,128,512]{2,1,0:T(8,128)(2,1)}, bf16[4,128,512]{2,1,0:T(8,128)(2,1)S(1)}, u32[]{:S(2)}, u32[]{:S(2)}) %collective-permute-start.22) | collective-permute-done | bytes 524320 | tf_op jit(solution)/shard_map/ppermute | solution.py:23
  160.9 12.9 %collective-permute-done.20 = bf16[4,128,512]{2,1,0:T(8,128)(2,1)S(1)} collective-permute-done((bf16[4,128,512]{2,1,0:T(8,128)(2,1)S(1)}, bf16[4,128,512]{2,1,0:T(8,128)(2,1)S(1)}, u32[]{:S(2)}, u32[]{:S(2)}) %collective-permute-start.20) | collective-permute-done | bytes 524320 | tf_op jit(solution)/shard_map/ppermute | solution.py:23
  174.1 10.9 %collective-permute-done.18 = bf16[8,64,512]{2,1,0:T(8,128)(2,1)S(1)} collective-permute-done((bf16[8,64,512]{2,1,0:T(8,128)(2,1)}, bf16[8,64,512]{2,1,0:T(8,128)(2,1)S(1)}, u32[]{:S(2)}, u32[]{:S(2)}) %collective-permute-start.18) | collective-permute-done | bytes 524320 | tf_op jit(solution)/shard_map/ppermute | solution.py:23
  187.9 18.0 %collective-permute-done.25 = bf16[8,128,512]{2,1,0:T(8,128)(2,1)S(1)} collective-permute-done((bf16[8,128,512]{2,1,0:T(8,128)(2,1)S(1)}, bf16[8,128,512]{2,1,0:T(8,128)(2,1)S(1)}, u32[]{:S(2)}, u32[]{:S(2)}) %collective-permute-start.25) | collective-permute-done | bytes 1048608 | tf_op jit(solution)/shard_map/ppermute | solution.py:23
  208.4 6.0 %collective-permute-start.27 = (bf16[8,64,512]{2,1,0:T(8,128)(2,1)}, bf16[8,64,512]{2,1,0:T(8,128)(2,1)}, u32[]{:S(2)}, u32[]{:S(2)}) collective-permute-start(bf16[8,64,512]{2,1,0:T(8,128)(2,1)} %get-tuple-element.138), channel_id=1, source_target_pairs={{0,16},{16,0},{32,48},{48,32},{64,80},{80,64},{96,112},{112,96},{1... | collective-permute-start | bytes 1572872 | tf_op jit(solution)/shard_map/ppermute | solution.py:23
  (107 shorter events, 31.2 us)
Async XLA Ops:
  18.3 77.8 %collective-permute-start.14 = (f32[2,16,512,128]{3,2,1,0:T(8,128)}, f32[2,16,512,128]{3,2,1,0:T(8,128)}, u32[]{:S(2)}, u32[]{:S(2)}) collective-permute-start(f32[2,16,512,128]{3,2,1,0:T(8,128)} %refs_10_.3), channel_id=1, source_target_pairs={{0,16},{16,0},{32,48},{48,32},{64,80},{80,64},{96,112},{112,96},{1... | collective-permute-start | bytes 25165832 | tf_op jit(solution)/shard_map/ppermute | solution.py:23
  18.5 44.9 %collective-permute-start.10 = (bf16[8,128,512]{2,1,0:T(8,128)(2,1)S(1)}, bf16[8,128,512]{2,1,0:T(8,128)(2,1)}, u32[]{:S(2)}, u32[]{:S(2)}) collective-permute-start(bf16[8,128,512]{2,1,0:T(8,128)(2,1)S(1)} %pad_maximum_fusion.refs_1_), channel_id=1, source_target_pairs={{0,192},{16,208},{32,224},{48,240},{64,0},{80,16},{96,32},{112,48}... | collective-permute-start | bytes 3145736 | tf_op jit(solution)/shard_map/ppermute | solution.py:23
  23.6 40.5 %collective-permute-start.11 = (bf16[8,128,512]{2,1,0:T(8,128)(2,1)S(1)}, bf16[8,128,512]{2,1,0:T(8,128)(2,1)}, u32[]{:S(2)}, u32[]{:S(2)}) collective-permute-start(bf16[8,128,512]{2,1,0:T(8,128)(2,1)S(1)} %pad_maximum_fusion.refs_1_), channel_id=1, source_target_pairs={{0,64},{16,80},{32,96},{48,112},{64,128},{80,144},{96,160},{112,17... | collective-permute-start | bytes 3145736 | tf_op jit(solution)/shard_map/ppermute | solution.py:23
  23.6 28.4 %collective-permute-start.2 = (bf16[4,128,512]{2,1,0:T(8,128)(2,1)S(1)}, bf16[4,128,512]{2,1,0:T(8,128)(2,1)S(1)}, u32[]{:S(2)}, u32[]{:S(2)}) collective-permute-start(bf16[4,128,512]{2,1,0:T(8,128)(2,1)S(1)} %fusion.10), channel_id=1, source_target_pairs={{0,32},{16,48},{32,0},{48,16},{64,96},{80,112},{96,64},{112,80},{1... | collective-permute-start | bytes 1572872 | tf_op jit(solution)/shard_map/ppermute | solution.py:23
  52.0 17.9 %collective-permute-start.3 = (bf16[4,128,512]{2,1,0:T(8,128)(2,1)S(1)}, bf16[4,128,512]{2,1,0:T(8,128)(2,1)S(1)}, u32[]{:S(2)}, u32[]{:S(2)}) collective-permute-start(bf16[4,128,512]{2,1,0:T(8,128)(2,1)S(1)} %collective-permute-done.2.refs_6_), channel_id=1, source_target_pairs={{0,192},{16,208},{32,224},{48,240},{64,0},{80,16},{96,32},{112,48}... | collective-permute-start | bytes 1572872 | tf_op jit(solution)/shard_map/ppermute | solution.py:23
  54.3 17.7 %collective-permute-start.4 = (bf16[4,128,512]{2,1,0:T(8,128)(2,1)S(1)}, bf16[4,128,512]{2,1,0:T(8,128)(2,1)S(1)}, u32[]{:S(2)}, u32[]{:S(2)}) collective-permute-start(bf16[4,128,512]{2,1,0:T(8,128)(2,1)S(1)} %collective-permute-done.2.refs_6_), channel_id=1, source_target_pairs={{0,128},{16,144},{32,160},{48,176},{64,192},{80,208},{96,224},{112... | collective-permute-start | bytes 1572872 | tf_op jit(solution)/shard_map/ppermute | solution.py:23
  63.5 16.9 %collective-permute-start.5 = (bf16[4,128,512]{2,1,0:T(8,128)(2,1)S(1)}, bf16[4,128,512]{2,1,0:T(8,128)(2,1)S(1)}, u32[]{:S(2)}, u32[]{:S(2)}) collective-permute-start(bf16[4,128,512]{2,1,0:T(8,128)(2,1)S(1)} %collective-permute-done.2.refs_6_), channel_id=1, source_target_pairs={{0,64},{16,80},{32,96},{48,112},{64,128},{80,144},{96,160},{112,17... | collective-permute-start | bytes 1572872 | tf_op jit(solution)/shard_map/ppermute | solution.py:23
  64.1 26.8 %collective-permute-start.6 = (bf16[4,128,512]{2,1,0:T(8,128)(2,1)S(1)}, bf16[4,128,512]{2,1,0:T(8,128)(2,1)S(1)}, u32[]{:S(2)}, u32[]{:S(2)}) collective-permute-start(bf16[4,128,512]{2,1,0:T(8,128)(2,1)S(1)} %slice.29), channel_id=1, source_target_pairs={{0,32},{16,48},{32,0},{48,16},{64,96},{80,112},{96,64},{112,80},{1... | collective-permute-start | bytes 1572872 | tf_op jit(solution)/shard_map/ppermute | solution.py:23
  69.9 26.3 %collective-permute-start.12 = (bf16[8,64,512]{2,1,0:T(8,128)(2,1)S(1)}, bf16[8,64,512]{2,1,0:T(8,128)(2,1)}, u32[]{:S(2)}, u32[]{:S(2)}) collective-permute-start(bf16[8,64,512]{2,1,0:T(8,128)(2,1)S(1)} %slice.30), channel_id=1, source_target_pairs={{0,192},{16,208},{32,224},{48,240},{64,0},{80,16},{96,32},{112,48}... | collective-permute-start | bytes 1572872 | tf_op jit(solution)/shard_map/ppermute | solution.py:23
  72.0 24.1 %collective-permute-start.13 = (bf16[8,64,512]{2,1,0:T(8,128)(2,1)S(1)}, bf16[8,64,512]{2,1,0:T(8,128)(2,1)}, u32[]{:S(2)}, u32[]{:S(2)}) collective-permute-start(bf16[8,64,512]{2,1,0:T(8,128)(2,1)S(1)} %slice.31), channel_id=1, source_target_pairs={{0,64},{16,80},{32,96},{48,112},{64,128},{80,144},{96,160},{112,17... | collective-permute-start | bytes 1572872 | tf_op jit(solution)/shard_map/ppermute | solution.py:23
  90.9 21.3 %collective-permute-start.7 = (bf16[4,128,512]{2,1,0:T(8,128)(2,1)S(1)}, bf16[4,128,512]{2,1,0:T(8,128)(2,1)S(1)}, u32[]{:S(2)}, u32[]{:S(2)}) collective-permute-start(bf16[4,128,512]{2,1,0:T(8,128)(2,1)S(1)} %collective-permute-done.6.refs_6_), channel_id=1, source_target_pairs={{0,192},{16,208},{32,224},{48,240},{64,0},{80,16},{96,32},{112,48}... | collective-permute-start | bytes 1572872 | tf_op jit(solution)/shard_map/ppermute | solution.py:23
  93.0 19.2 %collective-permute-start.8 = (bf16[4,128,512]{2,1,0:T(8,128)(2,1)S(1)}, bf16[4,128,512]{2,1,0:T(8,128)(2,1)}, u32[]{:S(2)}, u32[]{:S(2)}) collective-permute-start(bf16[4,128,512]{2,1,0:T(8,128)(2,1)S(1)} %collective-permute-done.6.refs_6_), channel_id=1, source_target_pairs={{0,128},{16,144},{32,160},{48,176},{64,192},{80,208},{96,224},{112... | collective-permute-start | bytes 1572872 | tf_op jit(solution)/shard_map/ppermute | solution.py:23
  96.1 23.5 %collective-permute-start.9 = (bf16[4,128,512]{2,1,0:T(8,128)(2,1)S(1)}, bf16[4,128,512]{2,1,0:T(8,128)(2,1)S(1)}, u32[]{:S(2)}, u32[]{:S(2)}) collective-permute-start(bf16[4,128,512]{2,1,0:T(8,128)(2,1)S(1)} %collective-permute-done.6.refs_6_), channel_id=1, source_target_pairs={{0,64},{16,80},{32,96},{48,112},{64,128},{80,144},{96,160},{112,17... | collective-permute-start | bytes 1572872 | tf_op jit(solution)/shard_map/ppermute | solution.py:23
  119.6 18.7 %collective-permute-start.17 = (bf16[4,128,512]{2,1,0:T(8,128)(2,1)}, bf16[4,128,512]{2,1,0:T(8,128)(2,1)S(1)}, u32[]{:S(2)}, u32[]{:S(2)}) collective-permute-start(bf16[4,128,512]{2,1,0:T(8,128)(2,1)} %get-tuple-element.102), channel_id=1, source_target_pairs={{0,192},{16,208},{32,224},{48,240},{64,0},{80,16},{96,32},{112,48}... | collective-permute-start | bytes 1572872 | tf_op jit(solution)/shard_map/ppermute | solution.py:23
  119.6 18.8 %collective-permute-start.16 = (bf16[4,128,512]{2,1,0:T(8,128)(2,1)}, bf16[4,128,512]{2,1,0:T(8,128)(2,1)S(1)}, u32[]{:S(2)}, u32[]{:S(2)}) collective-permute-start(bf16[4,128,512]{2,1,0:T(8,128)(2,1)} %get-tuple-element.101), channel_id=1, source_target_pairs={{0,128},{16,144},{32,160},{48,176},{64,192},{80,208},{96,224},{112... | collective-permute-start | bytes 1572872 | tf_op jit(solution)/shard_map/ppermute | solution.py:23
  121.5 25.0 %collective-permute-start.15 = (bf16[4,128,512]{2,1,0:T(8,128)(2,1)}, bf16[4,128,512]{2,1,0:T(8,128)(2,1)S(1)}, u32[]{:S(2)}, u32[]{:S(2)}) collective-permute-start(bf16[4,128,512]{2,1,0:T(8,128)(2,1)} %get-tuple-element.100), channel_id=1, source_target_pairs={{0,64},{16,80},{32,96},{48,112},{64,128},{80,144},{96,160},{112,17... | collective-permute-start | bytes 1572872 | tf_op jit(solution)/shard_map/ppermute | solution.py:23
  146.9 14.0 %collective-permute-start.21 = (bf16[4,128,512]{2,1,0:T(8,128)(2,1)S(1)}, bf16[4,128,512]{2,1,0:T(8,128)(2,1)S(1)}, u32[]{:S(2)}, u32[]{:S(2)}) collective-permute-start(bf16[4,128,512]{2,1,0:T(8,128)(2,1)S(1)} %copy-done.16), channel_id=1, source_target_pairs={{0,128},{16,144},{32,160},{48,176},{64,192},{80,208},{96,224},{112... | collective-permute-start | bytes 1572872 | tf_op jit(solution)/shard_map/ppermute | solution.py:23
  148.3 25.5 %collective-permute-start.20 = (bf16[4,128,512]{2,1,0:T(8,128)(2,1)S(1)}, bf16[4,128,512]{2,1,0:T(8,128)(2,1)S(1)}, u32[]{:S(2)}, u32[]{:S(2)}) collective-permute-start(bf16[4,128,512]{2,1,0:T(8,128)(2,1)S(1)} %copy-done.15), channel_id=1, source_target_pairs={{0,64},{16,80},{32,96},{48,112},{64,128},{80,144},{96,160},{112,17... | collective-permute-start | bytes 1572872 | tf_op jit(solution)/shard_map/ppermute | solution.py:23
  148.9 36.2 %collective-permute-start.18 = (bf16[8,64,512]{2,1,0:T(8,128)(2,1)}, bf16[8,64,512]{2,1,0:T(8,128)(2,1)S(1)}, u32[]{:S(2)}, u32[]{:S(2)}) collective-permute-start(bf16[8,64,512]{2,1,0:T(8,128)(2,1)} %get-tuple-element.123), channel_id=1, source_target_pairs={{0,64},{16,80},{32,96},{48,112},{64,128},{80,144},{96,160},{112,17... | collective-permute-start | bytes 1572872 | tf_op jit(solution)/shard_map/ppermute | solution.py:23
  149.9 35.2 %collective-permute-start.19 = (bf16[8,64,512]{2,1,0:T(8,128)(2,1)}, bf16[8,64,512]{2,1,0:T(8,128)(2,1)S(1)}, u32[]{:S(2)}, u32[]{:S(2)}) collective-permute-start(bf16[8,64,512]{2,1,0:T(8,128)(2,1)} %get-tuple-element.124), channel_id=1, source_target_pairs={{0,192},{16,208},{32,224},{48,240},{64,0},{80,16},{96,32},{112,48}... | collective-permute-start | bytes 1572872 | tf_op jit(solution)/shard_map/ppermute | solution.py:23
  160.1 25.0 %collective-permute-start.23 = (bf16[4,128,512]{2,1,0:T(8,128)(2,1)S(1)}, bf16[4,128,512]{2,1,0:T(8,128)(2,1)S(1)}, u32[]{:S(2)}, u32[]{:S(2)}) collective-permute-start(bf16[4,128,512]{2,1,0:T(8,128)(2,1)S(1)} %add_convert_fusion.3), channel_id=1, source_target_pairs={{0,32},{16,48},{32,0},{48,16},{64,96},{80,112},{96,64},{112,80},{1... | collective-permute-start | bytes 1572872 | tf_op jit(solution)/shard_map/ppermute | solution.py:23
  185.3 20.5 %collective-permute-start.25 = (bf16[8,128,512]{2,1,0:T(8,128)(2,1)S(1)}, bf16[8,128,512]{2,1,0:T(8,128)(2,1)S(1)}, u32[]{:S(2)}, u32[]{:S(2)}) collective-permute-start(bf16[8,128,512]{2,1,0:T(8,128)(2,1)S(1)} %add_convert_fusion), channel_id=1, source_target_pairs={{0,192},{16,208},{32,224},{48,240},{64,0},{80,16},{96,32},{112,48}... | collective-permute-start | bytes 3145736 | tf_op jit(solution)/shard_map/ppermute | solution.py:23
  185.6 20.9 %collective-permute-start.24 = (bf16[8,128,512]{2,1,0:T(8,128)(2,1)S(1)}, bf16[8,128,512]{2,1,0:T(8,128)(2,1)S(1)}, u32[]{:S(2)}, u32[]{:S(2)}) collective-permute-start(bf16[8,128,512]{2,1,0:T(8,128)(2,1)S(1)} %add_convert_fusion.1), channel_id=1, source_target_pairs={{0,64},{16,80},{32,96},{48,112},{64,128},{80,144},{96,160},{112,17... | collective-permute-start | bytes 3145736 | tf_op jit(solution)/shard_map/ppermute | solution.py:23
  187.1 19.8 %collective-permute-start.26 = (bf16[4,128,512]{2,1,0:T(8,128)(2,1)S(1)}, bf16[4,128,512]{2,1,0:T(8,128)(2,1)S(1)}, u32[]{:S(2)}, u32[]{:S(2)}) collective-permute-start(bf16[4,128,512]{2,1,0:T(8,128)(2,1)S(1)} %add_convert_fusion.2), channel_id=1, source_target_pairs={{0,32},{16,48},{32,0},{48,16},{64,96},{80,112},{96,64},{112,80},{1... | collective-permute-start | bytes 1572872 | tf_op jit(solution)/shard_map/ppermute | solution.py:23
  (23 other events, 381.1 us)

commit v3 on v2

--- a/solution.py
+++ b/solution.py
@@ -275,9 +275,10 @@
     far0 = to_far(pair[:step])
     above_o, below_o = to_last(pair), to_next(pair)
     shared = make_tables(later)
-    above_o, below_o, shared = tied(above_o, below_o, shared)
+    above_o, below_o, shared, far0, rim, pair = tied(
+        above_o, below_o, shared, far0, rim, pair
+    )
     low_o, high_o = relay(above_o, below_o)
-    far0, rim, pair = tied(far0, rim, pair)
     pieces = gather_ring(far0)
     gate = make_gate(short_weight, streams, rim)
     around = (pair, above_o, low_o, high_o, below_o)

time: 220 us -> 216 us (0.982)
  the two profiles are of different devices: /device:TPU:103 before, /device:TPU:68 now
where the time goes in v3:
time: 216 us; the launch traced here: 213 us
  waiting for transfers between devices  90.4 us (42%)
  starting transfers between devices  55.5 us (26%)
  Pallas kernels  41 us (19%)
  other arithmetic  13.9 us (6%)
  local copies, waits for them, and re-layouts  11.9 us (6%)
    ppermute x27, waiting for transfers between devices, send(): return lax.ppermute(block, 'ctx', [(i, target(i)) for i in range(16)])  90.4 us
    ppermute x27, starting transfers between devices, send(): return lax.ppermute(block, 'ctx', [(i, target(i)) for i in range(16)])  53.7 us
    pallas_call x2, Pallas kernels, convolve(): pl.pallas_call(lambda *refs: conv_kernel(count, *refs), grid_spec=pltpu.P...  32.2 us
    unnamed x40, local copies, waits for them, and re-layouts  7.3 us
    pallas_call x1, Pallas kernels, make_product(): pl.pallas_call(product_kernel, grid=(length // COLUMNS,), in_specs=[pl.Bl...  5.25 us
    another operation x1, other arithmetic  4.71 us
  transfers between devices with their start and end apart: 28, of which 13 were waited for; matrix products, arithmetic and copies ran while one was open for 8% of the time, Pallas kernels for 17%

profile of v3, /device:TPU:68, one launch (start us, length us, event | category | flops | bytes accessed | tf_op | source)
XLA Modules:
  0.0 213.0 jit_solution(15255604240741407497)
XLA Ops:
  4.4 5.2 %shard_map.64 = bf16[16,32768]{1,0:T(8,128)(2,1)} custom-call(bf16[3,16,3]{2,1,0:T(8,128)(2,1)} %copy.20.weight_ref, bf16[3,16,32768]{2,1,0:T(8,128)(2,1)} %second_last.1, bf16[3,16,32768]{2,1,0:T(8,128)(2,1)} %second_last.1, bf16[3,16,128]{2,1,0:T(8,128)(2,1)} %copy-done.8, bf16[3,16,32768]{2,1,0:T(8,128)(2,1)} %second_last.1, ...), custom_call_target="tpu_custom_call" | custom-call | flops 7340032 | bytes 3145728 | tf_op jit(solution)/shard_map/pallas_call | solution.py:93
  11.3 5.8 %collective-permute-start.1 = (bf16[8,64,512]{2,1,0:T(8,128)(2,1)S(1)}, bf16[8,64,512]{2,1,0:T(8,128)(2,1)S(1)}, u32[]{:S(2)}, u32[]{:S(2)}) collective-permute-start(bf16[8,64,512]{2,1,0:T(8,128)(2,1)S(1)} %get-tuple-element.142), channel_id=1, source_target_pairs={{0,16},{16,0},{32,48},{48,32},{64,80},{80,64},{96,112},{112,96},{1... | collective-permute-start | bytes 1572872 | tf_op jit(solution)/shard_map/ppermute | solution.py:23
  19.1 4.2 %collective-permute-start.2 = (bf16[8,128,512]{2,1,0:T(8,128)(2,1)S(1)}, bf16[8,128,512]{2,1,0:T(8,128)(2,1)}, u32[]{:S(2)}, u32[]{:S(2)}) collective-permute-start(bf16[8,128,512]{2,1,0:T(8,128)(2,1)S(1)} %pad_maximum_fusion.refs_1_), channel_id=1, source_target_pairs={{0,192},{16,208},{32,224},{48,240},{64,0},{80,16},{96,32},{112,48}... | collective-permute-start | bytes 3145736 | tf_op jit(solution)/shard_map/ppermute | solution.py:23
  23.9 4.5 %collective-permute-start.4 = (bf16[4,128,512]{2,1,0:T(8,128)(2,1)S(1)}, bf16[4,128,512]{2,1,0:T(8,128)(2,1)S(1)}, u32[]{:S(2)}, u32[]{:S(2)}) collective-permute-start(bf16[4,128,512]{2,1,0:T(8,128)(2,1)S(1)} %fusion.10), channel_id=1, source_target_pairs={{0,32},{16,48},{32,0},{48,16},{64,96},{80,112},{96,64},{112,80},{1... | collective-permute-start | bytes 1572872 | tf_op jit(solution)/shard_map/ppermute | solution.py:23
  28.6 4.7 %cosine_convert_fusion = (bf16[256,1024]{0,1:T(8,128)(2,1)S(1)}, bf16[256,1024]{0,1:T(8,128)(2,1)S(1)}) fusion(s32[1024]{0:T(1024)S(1)} %add.172, s32[256]{0:T(256)S(1)} %add_bitcast_fusion), kind=kLoop, calls=%fused_computation.26 | loop fusion | flops 4456448 | bytes 1053696 | tf_op jit(solution)/shard_map/convert
  34.4 3.2 %sine_negate_fusion = (f32[256,512]{1,0:T(8,128)}, f32[256,512]{1,0:T(8,128)}) fusion(s32[256]{0:T(256)S(1)} %add_bitcast_fusion), kind=kLoop, calls=%fused_computation.37 | loop fusion | flops 1966080 | bytes 1049600 | tf_op jit(solution)/shard_map/neg | solution.py:53
  37.7 15.2 %collective-permute-done.4.refs_6_ = bf16[4,128,512]{2,1,0:T(8,128)(2,1)S(1)} collective-permute-done((bf16[4,128,512]{2,1,0:T(8,128)(2,1)S(1)}, bf16[4,128,512]{2,1,0:T(8,128)(2,1)S(1)}, u32[]{:S(2)}, u32[]{:S(2)}) %collective-permute-start.4) | collective-permute-done | bytes 524320 | tf_op jit(solution)/shard_map/ppermute | solution.py:23
  56.9 4.5 %collective-permute-start.8 = (bf16[4,128,512]{2,1,0:T(8,128)(2,1)S(1)}, bf16[4,128,512]{2,1,0:T(8,128)(2,1)}, u32[]{:S(2)}, u32[]{:S(2)}) collective-permute-start(bf16[4,128,512]{2,1,0:T(8,128)(2,1)S(1)} %slice.29), channel_id=1, source_target_pairs={{0,32},{16,48},{32,0},{48,16},{64,96},{80,112},{96,64},{112,80},{1... | collective-permute-start | bytes 1572872 | tf_op jit(solution)/shard_map/ppermute | solution.py:23
  63.6 14.8 %collective-permute-done.5.refs_7_ = bf16[4,128,512]{2,1,0:T(8,128)(2,1)S(1)} collective-permute-done((bf16[4,128,512]{2,1,0:T(8,128)(2,1)S(1)}, bf16[4,128,512]{2,1,0:T(8,128)(2,1)S(1)}, u32[]{:S(2)}, u32[]{:S(2)}) %collective-permute-start.5) | collective-permute-done | bytes 524320 | tf_op jit(solution)/shard_map/ppermute | solution.py:23
  78.4 3.7 %collective-permute-start.12 = (bf16[8,64,512]{2,1,0:T(8,128)(2,1)S(1)}, bf16[8,64,512]{2,1,0:T(8,128)(2,1)}, u32[]{:S(2)}, u32[]{:S(2)}) collective-permute-start(bf16[8,64,512]{2,1,0:T(8,128)(2,1)S(1)} %slice.30), channel_id=1, source_target_pairs={{0,192},{16,208},{32,224},{48,240},{64,0},{80,16},{96,32},{112,48}... | collective-permute-start | bytes 1572872 | tf_op jit(solution)/shard_map/ppermute | solution.py:23
  84.2 3.5 %shard_map.65 = f32[16,32768]{1,0:T(8,128)} custom-call(bf16[3,16,3]{2,1,0:T(8,128)(2,1)} %copy.20.weight_ref, bf16[3,16,32768]{2,1,0:T(8,128)(2,1)} %second_last.1, bf16[3,16,32768]{2,1,0:T(8,128)(2,1)} %second_last.1, bf16[3,16,128]{2,1,0:T(8,128)(2,1)} %copy-done.8), custom_call_target="tpu_custom_call" | custom-call | flops 3670016 | bytes 3145728 | tf_op jit(solution)/shard_map/pallas_call | solution.py:110
  87.8 3.3 %collective-permute-start.9 = (bf16[4,128,512]{2,1,0:T(8,128)(2,1)}, bf16[4,128,512]{2,1,0:T(8,128)(2,1)S(1)}, u32[]{:S(2)}, u32[]{:S(2)}) collective-permute-start(bf16[4,128,512]{2,1,0:T(8,128)(2,1)} %collective-permute-done.8.refs_6_), channel_id=1, source_target_pairs={{0,192},{16,208},{32,224},{48,240},{64,0},{80,16},{96,32},{112,48}... | collective-permute-start | bytes 1572872 | tf_op jit(solution)/shard_map/ppermute | solution.py:23
  94.2 15.5 %collective-permute-done.13.refs_4_ = bf16[8,64,512]{2,1,0:T(8,128)(2,1)} collective-permute-done((bf16[8,64,512]{2,1,0:T(8,128)(2,1)S(1)}, bf16[8,64,512]{2,1,0:T(8,128)(2,1)}, u32[]{:S(2)}, u32[]{:S(2)}) %collective-permute-start.13) | collective-permute-done | bytes 524320 | tf_op jit(solution)/shard_map/ppermute | solution.py:23
  109.8 16.1 %shard_map.66 = (bf16[8,128,512]{2,1,0:T(8,128)(2,1)}, bf16[8,128,512]{2,1,0:T(8,128)(2,1)}, bf16[8,64,512]{2,1,0:T(8,128)(2,1)}, bf16[8,64,512]{2,1,0:T(8,128)(...) custom-call(s32[1]{0:T(128)} %bitcast.8.refs_0_, ...), custom_call_target="tpu_custom_call" | custom-call | flops 16106127360 | bytes 16777216 | tf_op jit(solution)/shard_map/pallas_call | solution.py:178
  128.0 16.1 %shard_map.67 = (bf16[8,128,512]{2,1,0:T(8,128)(2,1)}, bf16[8,128,512]{2,1,0:T(8,128)(2,1)}, bf16[8,64,512]{2,1,0:T(8,128)(2,1)}, bf16[8,64,512]{2,1,0:T(8,128)(...) custom-call(s32[1]{0:T(128)} %bitcast.8.refs_0_, ...), custom_call_target="tpu_custom_call", output_to_operand_aliasing={{0}: (18, {}), {1}: (19, {}), {2}: (20, {}), {3}: (21, {}),... | custom-call | flops 16106127360 | bytes 16777216 | tf_op jit(solution)/shard_map/pallas_call | solution.py:178
  144.2 5.9 %collective-permute-done.15 = bf16[4,128,512]{2,1,0:T(8,128)(2,1)S(1)} collective-permute-done((bf16[4,128,512]{2,1,0:T(8,128)(2,1)}, bf16[4,128,512]{2,1,0:T(8,128)(2,1)S(1)}, u32[]{:S(2)}, u32[]{:S(2)}) %collective-permute-start.15) | collective-permute-done | bytes 524320 | tf_op jit(solution)/shard_map/ppermute | solution.py:23
  155.8 8.0 %collective-permute-done.22 = bf16[4,128,512]{2,1,0:T(8,128)(2,1)S(1)} collective-permute-done((bf16[4,128,512]{2,1,0:T(8,128)(2,1)}, bf16[4,128,512]{2,1,0:T(8,128)(2,1)S(1)}, u32[]{:S(2)}, u32[]{:S(2)}) %collective-permute-start.22) | collective-permute-done | bytes 524320 | tf_op jit(solution)/shard_map/ppermute | solution.py:23
  163.9 4.6 %collective-permute-start.23 = (bf16[4,128,512]{2,1,0:T(8,128)(2,1)S(1)}, bf16[4,128,512]{2,1,0:T(8,128)(2,1)S(1)}, u32[]{:S(2)}, u32[]{:S(2)}) collective-permute-start(bf16[4,128,512]{2,1,0:T(8,128)(2,1)S(1)} %add_convert_fusion.3), channel_id=1, source_target_pairs={{0,32},{16,48},{32,0},{48,16},{64,96},{80,112},{96,64},{112,80},{1... | collective-permute-start | bytes 1572872 | tf_op jit(solution)/shard_map/ppermute | solution.py:23
  171.4 5.3 %collective-permute-done.18 = bf16[8,64,512]{2,1,0:T(8,128)(2,1)S(1)} collective-permute-done((bf16[8,64,512]{2,1,0:T(8,128)(2,1)}, bf16[8,64,512]{2,1,0:T(8,128)(2,1)S(1)}, u32[]{:S(2)}, u32[]{:S(2)}) %collective-permute-start.18) | collective-permute-done | bytes 524320 | tf_op jit(solution)/shard_map/ppermute | solution.py:23
  176.7 4.9 %collective-permute-done.23 = bf16[4,128,512]{2,1,0:T(8,128)(2,1)S(1)} collective-permute-done((bf16[4,128,512]{2,1,0:T(8,128)(2,1)S(1)}, bf16[4,128,512]{2,1,0:T(8,128)(2,1)S(1)}, u32[]{:S(2)}, u32[]{:S(2)}) %collective-permute-start.23) | collective-permute-done | bytes 524320 | tf_op jit(solution)/shard_map/ppermute | solution.py:23
  181.7 4.0 %collective-permute-start.25 = (bf16[8,128,512]{2,1,0:T(8,128)(2,1)S(1)}, bf16[8,128,512]{2,1,0:T(8,128)(2,1)S(1)}, u32[]{:S(2)}, u32[]{:S(2)}) collective-permute-start(bf16[8,128,512]{2,1,0:T(8,128)(2,1)S(1)} %add_convert_fusion), channel_id=1, source_target_pairs={{0,192},{16,208},{32,224},{48,240},{64,0},{80,16},{96,32},{112,48}... | collective-permute-start | bytes 3145736 | tf_op jit(solution)/shard_map/ppermute | solution.py:23
  186.0 7.2 %collective-permute-start.26 = (bf16[4,128,512]{2,1,0:T(8,128)(2,1)S(1)}, bf16[4,128,512]{2,1,0:T(8,128)(2,1)S(1)}, u32[]{:S(2)}, u32[]{:S(2)}) collective-permute-start(bf16[4,128,512]{2,1,0:T(8,128)(2,1)S(1)} %add_convert_fusion.2), channel_id=1, source_target_pairs={{0,32},{16,48},{32,0},{48,16},{64,96},{80,112},{96,64},{112,80},{1... | collective-permute-start | bytes 1572872 | tf_op jit(solution)/shard_map/ppermute | solution.py:23
  193.2 9.1 %collective-permute-done.25 = bf16[8,128,512]{2,1,0:T(8,128)(2,1)S(1)} collective-permute-done((bf16[8,128,512]{2,1,0:T(8,128)(2,1)S(1)}, bf16[8,128,512]{2,1,0:T(8,128)(2,1)S(1)}, u32[]{:S(2)}, u32[]{:S(2)}) %collective-permute-start.25) | collective-permute-done | bytes 1048608 | tf_op jit(solution)/shard_map/ppermute | solution.py:23
  202.3 3.7 %collective-permute-done.24 = bf16[8,128,512]{2,1,0:T(8,128)(2,1)S(1)} collective-permute-done((bf16[8,128,512]{2,1,0:T(8,128)(2,1)S(1)}, bf16[8,128,512]{2,1,0:T(8,128)(2,1)S(1)}, u32[]{:S(2)}, u32[]{:S(2)}) %collective-permute-start.24) | collective-permute-done | bytes 1048608 | tf_op jit(solution)/shard_map/ppermute | solution.py:23
  (105 shorter events, 39.4 us)
Async XLA Ops:
  18.6 91.1 %collective-permute-start.14 = (f32[2,16,512,128]{3,2,1,0:T(8,128)}, f32[2,16,512,128]{3,2,1,0:T(8,128)}, u32[]{:S(2)}, u32[]{:S(2)}) collective-permute-start(f32[2,16,512,128]{3,2,1,0:T(8,128)} %refs_10_.3), channel_id=1, source_target_pairs={{0,16},{16,0},{32,48},{48,32},{64,80},{80,64},{96,112},{112,96},{1... | collective-permute-start | bytes 25165832 | tf_op jit(solution)/shard_map/ppermute | solution.py:23
  19.1 33.8 %collective-permute-start.2 = (bf16[8,128,512]{2,1,0:T(8,128)(2,1)S(1)}, bf16[8,128,512]{2,1,0:T(8,128)(2,1)}, u32[]{:S(2)}, u32[]{:S(2)}) collective-permute-start(bf16[8,128,512]{2,1,0:T(8,128)(2,1)S(1)} %pad_maximum_fusion.refs_1_), channel_id=1, source_target_pairs={{0,192},{16,208},{32,224},{48,240},{64,0},{80,16},{96,32},{112,48}... | collective-permute-start | bytes 3145736 | tf_op jit(solution)/shard_map/ppermute | solution.py:23
  23.3 29.6 %collective-permute-start.3 = (bf16[8,128,512]{2,1,0:T(8,128)(2,1)S(1)}, bf16[8,128,512]{2,1,0:T(8,128)(2,1)}, u32[]{:S(2)}, u32[]{:S(2)}) collective-permute-start(bf16[8,128,512]{2,1,0:T(8,128)(2,1)S(1)} %pad_maximum_fusion.refs_1_), channel_id=1, source_target_pairs={{0,64},{16,80},{32,96},{48,112},{64,128},{80,144},{96,160},{112,17... | collective-permute-start | bytes 3145736 | tf_op jit(solution)/shard_map/ppermute | solution.py:23
  23.9 29.0 %collective-permute-start.4 = (bf16[4,128,512]{2,1,0:T(8,128)(2,1)S(1)}, bf16[4,128,512]{2,1,0:T(8,128)(2,1)S(1)}, u32[]{:S(2)}, u32[]{:S(2)}) collective-permute-start(bf16[4,128,512]{2,1,0:T(8,128)(2,1)S(1)} %fusion.10), channel_id=1, source_target_pairs={{0,32},{16,48},{32,0},{48,16},{64,96},{80,112},{96,64},{112,80},{1... | collective-permute-start | bytes 1572872 | tf_op jit(solution)/shard_map/ppermute | solution.py:23
  52.9 25.5 %collective-permute-start.5 = (bf16[4,128,512]{2,1,0:T(8,128)(2,1)S(1)}, bf16[4,128,512]{2,1,0:T(8,128)(2,1)S(1)}, u32[]{:S(2)}, u32[]{:S(2)}) collective-permute-start(bf16[4,128,512]{2,1,0:T(8,128)(2,1)S(1)} %collective-permute-done.4.refs_6_), channel_id=1, source_target_pairs={{0,192},{16,208},{32,224},{48,240},{64,0},{80,16},{96,32},{112,48}... | collective-permute-start | bytes 1572872 | tf_op jit(solution)/shard_map/ppermute | solution.py:23
  55.9 26.1 %collective-permute-start.6 = (bf16[4,128,512]{2,1,0:T(8,128)(2,1)S(1)}, bf16[4,128,512]{2,1,0:T(8,128)(2,1)S(1)}, u32[]{:S(2)}, u32[]{:S(2)}) collective-permute-start(bf16[4,128,512]{2,1,0:T(8,128)(2,1)S(1)} %collective-permute-done.4.refs_6_), channel_id=1, source_target_pairs={{0,128},{16,144},{32,160},{48,176},{64,192},{80,208},{96,224},{112... | collective-permute-start | bytes 1572872 | tf_op jit(solution)/shard_map/ppermute | solution.py:23
  55.9 31.8 %collective-permute-start.7 = (bf16[4,128,512]{2,1,0:T(8,128)(2,1)S(1)}, bf16[4,128,512]{2,1,0:T(8,128)(2,1)}, u32[]{:S(2)}, u32[]{:S(2)}) collective-permute-start(bf16[4,128,512]{2,1,0:T(8,128)(2,1)S(1)} %collective-permute-done.4.refs_6_), channel_id=1, source_target_pairs={{0,64},{16,80},{32,96},{48,112},{64,128},{80,144},{96,160},{112,17... | collective-permute-start | bytes 1572872 | tf_op jit(solution)/shard_map/ppermute | solution.py:23
  56.9 30.8 %collective-permute-start.8 = (bf16[4,128,512]{2,1,0:T(8,128)(2,1)S(1)}, bf16[4,128,512]{2,1,0:T(8,128)(2,1)}, u32[]{:S(2)}, u32[]{:S(2)}) collective-permute-start(bf16[4,128,512]{2,1,0:T(8,128)(2,1)S(1)} %slice.29), channel_id=1, source_target_pairs={{0,32},{16,48},{32,0},{48,16},{64,96},{80,112},{96,64},{112,80},{1... | collective-permute-start | bytes 1572872 | tf_op jit(solution)/shard_map/ppermute | solution.py:23
  78.4 15.8 %collective-permute-start.12 = (bf16[8,64,512]{2,1,0:T(8,128)(2,1)S(1)}, bf16[8,64,512]{2,1,0:T(8,128)(2,1)}, u32[]{:S(2)}, u32[]{:S(2)}) collective-permute-start(bf16[8,64,512]{2,1,0:T(8,128)(2,1)S(1)} %slice.30), channel_id=1, source_target_pairs={{0,192},{16,208},{32,224},{48,240},{64,0},{80,16},{96,32},{112,48}... | collective-permute-start | bytes 1572872 | tf_op jit(solution)/shard_map/ppermute | solution.py:23
  82.9 26.9 %collective-permute-start.13 = (bf16[8,64,512]{2,1,0:T(8,128)(2,1)S(1)}, bf16[8,64,512]{2,1,0:T(8,128)(2,1)}, u32[]{:S(2)}, u32[]{:S(2)}) collective-permute-start(bf16[8,64,512]{2,1,0:T(8,128)(2,1)S(1)} %slice.31), channel_id=1, source_target_pairs={{0,64},{16,80},{32,96},{48,112},{64,128},{80,144},{96,160},{112,17... | collective-permute-start | bytes 1572872 | tf_op jit(solution)/shard_map/ppermute | solution.py:23
  87.8 38.1 %collective-permute-start.9 = (bf16[4,128,512]{2,1,0:T(8,128)(2,1)}, bf16[4,128,512]{2,1,0:T(8,128)(2,1)S(1)}, u32[]{:S(2)}, u32[]{:S(2)}) collective-permute-start(bf16[4,128,512]{2,1,0:T(8,128)(2,1)} %collective-permute-done.8.refs_6_), channel_id=1, source_target_pairs={{0,192},{16,208},{32,224},{48,240},{64,0},{80,16},{96,32},{112,48}... | collective-permute-start | bytes 1572872 | tf_op jit(solution)/shard_map/ppermute | solution.py:23
  91.1 34.8 %collective-permute-start.10 = (bf16[4,128,512]{2,1,0:T(8,128)(2,1)}, bf16[4,128,512]{2,1,0:T(8,128)(2,1)S(1)}, u32[]{:S(2)}, u32[]{:S(2)}) collective-permute-start(bf16[4,128,512]{2,1,0:T(8,128)(2,1)} %collective-permute-done.8.refs_6_), channel_id=1, source_target_pairs={{0,128},{16,144},{32,160},{48,176},{64,192},{80,208},{96,224},{112... | collective-permute-start | bytes 1572872 | tf_op jit(solution)/shard_map/ppermute | solution.py:23
  94.2 31.7 %collective-permute-start.11 = (bf16[4,128,512]{2,1,0:T(8,128)(2,1)}, bf16[4,128,512]{2,1,0:T(8,128)(2,1)S(1)}, u32[]{:S(2)}, u32[]{:S(2)}) collective-permute-start(bf16[4,128,512]{2,1,0:T(8,128)(2,1)} %collective-permute-done.8.refs_6_), channel_id=1, source_target_pairs={{0,64},{16,80},{32,96},{48,112},{64,128},{80,144},{96,160},{112,17... | collective-permute-start | bytes 1572872 | tf_op jit(solution)/shard_map/ppermute | solution.py:23
  125.9 18.3 %collective-permute-start.17 = (bf16[4,128,512]{2,1,0:T(8,128)(2,1)}, bf16[4,128,512]{2,1,0:T(8,128)(2,1)S(1)}, u32[]{:S(2)}, u32[]{:S(2)}) collective-permute-start(bf16[4,128,512]{2,1,0:T(8,128)(2,1)} %get-tuple-element.102), channel_id=1, source_target_pairs={{0,192},{16,208},{32,224},{48,240},{64,0},{80,16},{96,32},{112,48}... | collective-permute-start | bytes 1572872 | tf_op jit(solution)/shard_map/ppermute | solution.py:23
  126.0 18.2 %collective-permute-start.16 = (bf16[4,128,512]{2,1,0:T(8,128)(2,1)}, bf16[4,128,512]{2,1,0:T(8,128)(2,1)S(1)}, u32[]{:S(2)}, u32[]{:S(2)}) collective-permute-start(bf16[4,128,512]{2,1,0:T(8,128)(2,1)} %get-tuple-element.101), channel_id=1, source_target_pairs={{0,128},{16,144},{32,160},{48,176},{64,192},{80,208},{96,224},{112... | collective-permute-start | bytes 1572872 | tf_op jit(solution)/shard_map/ppermute | solution.py:23
  126.1 24.0 %collective-permute-start.15 = (bf16[4,128,512]{2,1,0:T(8,128)(2,1)}, bf16[4,128,512]{2,1,0:T(8,128)(2,1)S(1)}, u32[]{:S(2)}, u32[]{:S(2)}) collective-permute-start(bf16[4,128,512]{2,1,0:T(8,128)(2,1)} %get-tuple-element.100), channel_id=1, source_target_pairs={{0,64},{16,80},{32,96},{48,112},{64,128},{80,144},{96,160},{112,17... | collective-permute-start | bytes 1572872 | tf_op jit(solution)/shard_map/ppermute | solution.py:23
  150.5 18.0 %collective-permute-start.21 = (bf16[4,128,512]{2,1,0:T(8,128)(2,1)S(1)}, bf16[4,128,512]{2,1,0:T(8,128)(2,1)S(1)}, u32[]{:S(2)}, u32[]{:S(2)}) collective-permute-start(bf16[4,128,512]{2,1,0:T(8,128)(2,1)S(1)} %copy-done.15), channel_id=1, source_target_pairs={{0,128},{16,144},{32,160},{48,176},{64,192},{80,208},{96,224},{112... | collective-permute-start | bytes 1572872 | tf_op jit(solution)/shard_map/ppermute | solution.py:23
  150.9 20.2 %collective-permute-start.20 = (bf16[4,128,512]{2,1,0:T(8,128)(2,1)S(1)}, bf16[4,128,512]{2,1,0:T(8,128)(2,1)S(1)}, u32[]{:S(2)}, u32[]{:S(2)}) collective-permute-start(bf16[4,128,512]{2,1,0:T(8,128)(2,1)S(1)} %copy-done.12), channel_id=1, source_target_pairs={{0,64},{16,80},{32,96},{48,112},{64,128},{80,144},{96,160},{112,17... | collective-permute-start | bytes 1572872 | tf_op jit(solution)/shard_map/ppermute | solution.py:23
  152.6 24.1 %collective-permute-start.18 = (bf16[8,64,512]{2,1,0:T(8,128)(2,1)}, bf16[8,64,512]{2,1,0:T(8,128)(2,1)S(1)}, u32[]{:S(2)}, u32[]{:S(2)}) collective-permute-start(bf16[8,64,512]{2,1,0:T(8,128)(2,1)} %get-tuple-element.123), channel_id=1, source_target_pairs={{0,64},{16,80},{32,96},{48,112},{64,128},{80,144},{96,160},{112,17... | collective-permute-start | bytes 1572872 | tf_op jit(solution)/shard_map/ppermute | solution.py:23
  154.3 22.4 %collective-permute-start.19 = (bf16[8,64,512]{2,1,0:T(8,128)(2,1)}, bf16[8,64,512]{2,1,0:T(8,128)(2,1)S(1)}, u32[]{:S(2)}, u32[]{:S(2)}) collective-permute-start(bf16[8,64,512]{2,1,0:T(8,128)(2,1)} %get-tuple-element.124), channel_id=1, source_target_pairs={{0,192},{16,208},{32,224},{48,240},{64,0},{80,16},{96,32},{112,48}... | collective-permute-start | bytes 1572872 | tf_op jit(solution)/shard_map/ppermute | solution.py:23
  163.9 17.7 %collective-permute-start.23 = (bf16[4,128,512]{2,1,0:T(8,128)(2,1)S(1)}, bf16[4,128,512]{2,1,0:T(8,128)(2,1)S(1)}, u32[]{:S(2)}, u32[]{:S(2)}) collective-permute-start(bf16[4,128,512]{2,1,0:T(8,128)(2,1)S(1)} %add_convert_fusion.3), channel_id=1, source_target_pairs={{0,32},{16,48},{32,0},{48,16},{64,96},{80,112},{96,64},{112,80},{1... | collective-permute-start | bytes 1572872 | tf_op jit(solution)/shard_map/ppermute | solution.py:23
  181.7 20.6 %collective-permute-start.25 = (bf16[8,128,512]{2,1,0:T(8,128)(2,1)S(1)}, bf16[8,128,512]{2,1,0:T(8,128)(2,1)S(1)}, u32[]{:S(2)}, u32[]{:S(2)}) collective-permute-start(bf16[8,128,512]{2,1,0:T(8,128)(2,1)S(1)} %add_convert_fusion), channel_id=1, source_target_pairs={{0,192},{16,208},{32,224},{48,240},{64,0},{80,16},{96,32},{112,48}... | collective-permute-start | bytes 3145736 | tf_op jit(solution)/shard_map/ppermute | solution.py:23
  185.9 20.1 %collective-permute-start.24 = (bf16[8,128,512]{2,1,0:T(8,128)(2,1)S(1)}, bf16[8,128,512]{2,1,0:T(8,128)(2,1)S(1)}, u32[]{:S(2)}, u32[]{:S(2)}) collective-permute-start(bf16[8,128,512]{2,1,0:T(8,128)(2,1)S(1)} %add_convert_fusion.1), channel_id=1, source_target_pairs={{0,64},{16,80},{32,96},{48,112},{64,128},{80,144},{96,160},{112,17... | collective-permute-start | bytes 3145736 | tf_op jit(solution)/shard_map/ppermute | solution.py:23
  186.0 20.4 %collective-permute-start.26 = (bf16[4,128,512]{2,1,0:T(8,128)(2,1)S(1)}, bf16[4,128,512]{2,1,0:T(8,128)(2,1)S(1)}, u32[]{:S(2)}, u32[]{:S(2)}) collective-permute-start(bf16[4,128,512]{2,1,0:T(8,128)(2,1)S(1)} %add_convert_fusion.2), channel_id=1, source_target_pairs={{0,32},{16,48},{32,0},{48,16},{64,96},{80,112},{96,64},{112,80},{1... | collective-permute-start | bytes 1572872 | tf_op jit(solution)/shard_map/ppermute | solution.py:23
  (22 other events, 292.4 us)
